TPU v7x, 32 devices: a whole 2x2x4 slice. The times are simulated.
32 devices in a mesh: groups: 2 (over y), tile: 4 (over x, core), member: 4 (over z).
Axes of the slice: x: 2, y: 2, z: 4, core: 2. Of those that a mesh axis runs over, the one named last changes fastest.
Arguments:
- fields: bfloat16 [8, 6, 16, 16, 256], P(('groups', 'member'), None, 'tile'), parts along dimension 0, may hold values from -6 to 6
- weight: bfloat16 [2304, 256], P(('tile', 'member')), may hold values from -0.125 to 0.125
- cotangent: bfloat16 [8, 6, 16, 16, 256], P(('groups', 'member'), None, 'tile'), parts along dimension 0, may hold values from -6 to 6
- adjacency: int32 [6, 4, 3], replicated, may hold values from 0 to 5, as said below
Outputs:
- activation: bfloat16 [8, 6, 16, 16, 256], P(('groups', 'member'), None, 'tile'), parts along dimension 0
- input_grad: bfloat16 [8, 6, 16, 16, 256], P(('groups', 'member'), None, 'tile'), parts along dimension 0
- weight_grad: float32 [4608, 256], P(('groups', 'tile', 'member')), parts along dimension 0
There are 2 independent parts, one for each index of `groups`. A program takes and returns all parts, laid end to end along the dimension named above; an argument that names none is the same for every part. Nothing has to cross between parts.
Inputs may be any that keep to these rules, and one draw needn't show every extreme that they name: `adjacency`: each row names a face other than f, an edge 0 to 3 of it and a flag 0 or 1; the pairing is symmetric (edge e of f names edge k of g exactly when edge k of g names edge e of f, with the same flag) and sews the six faces into the surface of a cube.
All inputs are finite; a program needn't handle non-finite values.
Results may differ from a plain program's by a relative error of at most 0.005.
Values may be sent and summed in bfloat16 or wider, within the bound.
A program may use at most 128 MiB of HBM per device.

v0:
```python
import math

import jax
import jax.numpy as jnp
from jax import lax
from jax.sharding import PartitionSpec as P

gelu_scale = 0.7978845608028654


def from_root(value, axis, source):
    kept = jnp.where(lax.axis_index(axis) == source, value, 0).astype(value.dtype)
    return lax.psum(kept, axis)


def extended(cells, sides, width):
    for axis, dim in sides:
        count = lax.axis_size(axis)
        ends = count - 1
        head = lax.slice_in_dim(cells, 0, width, axis=dim)
        tail = lax.slice_in_dim(cells, cells.shape[dim] - width, cells.shape[dim], axis=dim)
        cells = jnp.concatenate(
            [
                lax.ppermute(tail, axis, [(i, (i + 1) % count) for i in range(ends)]),
                cells,
                lax.ppermute(head, axis, [((i + 1) % count, i) for i in range(ends)]),
            ],
            axis=dim,
        )
    return cells


def gelu_tanh(argument):
    return (
        0.5
        * argument
        * (1.0 + jnp.tanh(gelu_scale * (argument + 0.044715 * argument * argument * argument)))
    )


def edge_selector(adjacency):
    source_index = adjacency[:, :, 2] * 24 + adjacency[:, :, 0] * 4 + adjacency[:, :, 1]
    source_index = source_index.reshape(24)
    return (source_index[:, None] == jnp.arange(48, dtype=jnp.int32)[None, :]).astype(jnp.float32)


def route_lines(cycle_grad, selector):
    members, face_count, edges, face_size, channels = cycle_grad.shape
    flat_cycle = cycle_grad.reshape(members, 24, face_size, channels)
    routed = jnp.einsum("ts,mtfc->msfc", selector, flat_cycle, precision=lax.Precision.HIGHEST)
    line_grad = routed[:, :24] + routed[:, 24:, ::-1]
    return line_grad.reshape(members, face_count, 4, face_size, channels)


def shards(fields, weight, cotangent, adjacency):
    members, face_count, band_rows, face_size, channels = fields.shape
    position = lax.axis_index("tile")
    tile_count = lax.axis_size("tile")
    top_device = position == 0
    bottom_device = position == tile_count - 1
    row_start = position * band_rows
    selector = edge_selector(adjacency)
    full_weight = lax.all_gather(weight, ("tile", "member"), axis=0, tiled=True)
    side_columns = jnp.stack([fields[:, :, :, 0, :], fields[:, :, :, -1, :]], axis=2)
    all_columns = lax.all_gather(side_columns, "tile", axis=3, tiled=True)
    north_lines = from_root(fields[:, :, 0, :, :], "tile", 0)
    south_lines = from_root(fields[:, :, -1, :, :], "tile", tile_count - 1)
    edge_lines = jnp.concatenate(
        [north_lines[:, :, None], south_lines[:, :, None], all_columns], axis=2
    )
    edge_lines = edge_lines.reshape(members, 24, face_size, channels)
    both_ways = jnp.concatenate([edge_lines, edge_lines[:, :, ::-1]], axis=1)
    cycle_cells = jnp.einsum(
        "ts,msfc->mtfc",
        selector.astype(jnp.bfloat16),
        both_ways,
        preferred_element_type=jnp.float32,
    )
    cycle_cells = cycle_cells.astype(jnp.bfloat16).reshape(
        members, face_count, 4, face_size, channels
    )
    side_cycle = lax.dynamic_slice_in_dim(cycle_cells[:, :, 2:4], row_start, band_rows, 3)
    widened = jnp.concatenate(
        [side_cycle[:, :, 0][:, :, :, None], fields, side_cycle[:, :, 1][:, :, :, None]], axis=3
    )
    padded = extended(widened, (("tile", 2),), 1)
    zero_cell = jnp.zeros((members, face_count, 1, channels), jnp.bfloat16)
    north_row = jnp.concatenate([zero_cell, cycle_cells[:, :, 0], zero_cell], axis=2)
    south_row = jnp.concatenate([zero_cell, cycle_cells[:, :, 1], zero_cell], axis=2)
    padded = padded.at[:, :, 0].set(jnp.where(top_device, north_row, padded[:, :, 0]))
    padded = padded.at[:, :, -1].set(jnp.where(bottom_device, south_row, padded[:, :, -1]))
    cell_count = members * face_count * band_rows * face_size
    pre_act = jnp.zeros((cell_count, channels), jnp.float32)
    for row_step in range(3):
        for col_step in range(3):
            offset = 3 * row_step + col_step
            window = padded[
                :, :, row_step : row_step + band_rows, col_step : col_step + face_size
            ].reshape(cell_count, channels)
            pre_act = pre_act + jnp.dot(
                window,
                full_weight[offset * channels : (offset + 1) * channels],
                preferred_element_type=jnp.float32,
            )
    activation = gelu_tanh(pre_act).astype(jnp.bfloat16).reshape(fields.shape)
    unused_value, pullback = jax.vjp(gelu_tanh, pre_act)
    act_grad = pullback(cotangent.reshape(cell_count, channels).astype(jnp.float32))[0].astype(
        jnp.bfloat16
    )
    grad_terms = []
    grad_pad = jnp.zeros((members, face_count, band_rows + 2, face_size + 2, channels), jnp.float32)
    for row_step in range(3):
        for col_step in range(3):
            offset = 3 * row_step + col_step
            window = padded[
                :, :, row_step : row_step + band_rows, col_step : col_step + face_size
            ].reshape(cell_count, channels)
            grad_terms.append(
                lax.dot_general(
                    window, act_grad, (((0,), (0,)), ((), ())), preferred_element_type=jnp.float32
                )
            )
            kernel_rows = full_weight[offset * channels : (offset + 1) * channels]
            product_term = jnp.dot(act_grad, kernel_rows.T, preferred_element_type=jnp.float32)
            product_term = product_term.reshape(members, face_count, band_rows, face_size, channels)
            grad_pad = grad_pad.at[
                :, :, row_step : row_step + band_rows, col_step : col_step + face_size
            ].add(product_term)
    local_grad = jnp.concatenate(grad_terms, axis=0)
    owned_rows = lax.psum_scatter(local_grad, ("tile", "member"), scatter_dimension=0, tiled=True)
    total_cells = cell_count * tile_count * lax.axis_size("member")
    weight_grad = owned_rows / math.sqrt(total_cells)
    cycle_rows = jnp.stack([grad_pad[:, :, 0], grad_pad[:, :, -1]], axis=2)
    received = extended(cycle_rows, (("tile", 2),), 1)
    band_grad = grad_pad[:, :, 1:-1]
    band_grad = band_grad.at[:, :, 0].add(received[:, :, 0])
    band_grad = band_grad.at[:, :, -1].add(received[:, :, 3])
    side_grad = jnp.stack([band_grad[:, :, :, 0], band_grad[:, :, :, -1]], axis=2)
    side_full = lax.dynamic_update_slice_in_dim(
        jnp.zeros((members, face_count, 2, face_size, channels), jnp.float32),
        side_grad,
        row_start,
        3,
    )
    north_grad = jnp.where(top_device, grad_pad[:, :, 0, 1:-1], 0.0)
    south_grad = jnp.where(bottom_device, grad_pad[:, :, -1, 1:-1], 0.0)
    cycle_grad = jnp.concatenate(
        [north_grad[:, :, None], south_grad[:, :, None], side_full], axis=2
    )
    line_grad = route_lines(cycle_grad, selector)
    side_share = lax.psum_scatter(
        line_grad[:, :, 2:4].astype(jnp.bfloat16), "tile", scatter_dimension=3, tiled=True
    ).astype(jnp.float32)
    top_bottom = lax.psum(line_grad[:, :, 0:2].astype(jnp.bfloat16), "tile").astype(jnp.float32)
    cell_grad = band_grad[:, :, :, 1:-1]
    cell_grad = cell_grad.at[:, :, :, 0].add(side_share[:, :, 0])
    cell_grad = cell_grad.at[:, :, :, -1].add(side_share[:, :, 1])
    cell_grad = cell_grad.at[:, :, 0].add(jnp.where(top_device, top_bottom[:, :, 0], 0.0))
    cell_grad = cell_grad.at[:, :, -1].add(jnp.where(bottom_device, top_bottom[:, :, 1], 0.0))
    input_grad = cell_grad.astype(jnp.bfloat16)
    return (activation, input_grad, weight_grad)


def solution(mesh):
    in_specs = (
        P(("groups", "member"), None, "tile", None, None),
        P(("tile", "member"), None),
        P(("groups", "member"), None, "tile", None, None),
        P(),
    )
    out_specs = (
        P(("groups", "member"), None, "tile", None, None),
        P(("groups", "member"), None, "tile", None, None),
        P(("groups", "tile", "member"), None),
    )
    return jax.shard_map(shards, mesh=mesh, in_specs=in_specs, out_specs=out_specs, check_vma=False)
```

profile of v0, /device:TPU:0, one launch (start us, length us, event | category | flops | bytes accessed | tf_op | source)
XLA Modules:
  0.0 224.5 jit_solution(6184690400154656035)
XLA Ops:
  8.1 0.8 fusion.62
  8.9 0.9 broadcast_select_fusion.2
  9.9 0.5 all-gather.2.cloned.1.call-update
  10.4 1.0 fusion.63
  11.5 0.7 slice_add_fusion.9
  12.4 6.3 %all_gather.6 = bf16[1,6,2,16,256]{4,2,1,0,3:T(2,128)(2,1)S(1)} all-gather(bf16[1,6,2,4,256]{4,2,1,0,3:T(2,128)(2,1)S(1)} %copy.128), channel_id=1, replica_groups=mesh['groups'=2,'tile'=4,'member'=4] {'tile'}, dimensions={3}, use_global_device_ids=true | all-gather | bytes 122880 | tf_op jit(solution)/shard_map/all_gather | solution.py:65
  18.7 0.6 fusion.65
  19.3 0.6 fusion.64
  19.9 0.7 and_reduce_fusion
  20.6 27.5 %all-reduce.7.cloned.1.call-done = (bf16[1,6,1,16,256]{4,2,1,3,0:T(2,128)(2,1)}, bf16[1,6,1,16,256]{4,2,1,3,0:T(2,128)(2,1)}) async-done(((bf16[1,6,1,16,256]{4,2,1,3,0:T(2,128)(2,1)}, bf16[1,6,1,16,256]{4,2,1,3,0:T(2,128)(2,1)}), (bf16[1,6,1,16,256]{4,2,1,3,0:T(2,128)(2,1)}, bf16[1,6,1,16,256]{4,2,1,3,0:T(2,128)(2,1)})) %all-reduce.7.cloned.1.call-update) | async-done | bytes 98320 | tf_op jit(solution)/shard_map/psum | solution.py:13
  48.0 1.3 pad_maximum_fusion.2
  50.3 1.3 collective-permute-start.1
  51.6 3.0 %collective-permute-start = (bf16[1,6,1,18,256]{4,3,2,1,0:T(8,128)(2,1)S(1)}, bf16[1,6,1,18,256]{4,3,2,1,0:T(8,128)(2,1)S(1)}, u32[]{:S(2)}, u32[]{:S(2)}) collective-permute-start(bf16[1,6,1,18,256]{4,3,2,1,0:T(8,128)(2,1)S(1)} %get-tuple-element.240), channel_id=1, source_target_pairs={{0,4},{4,8},{8,12},{1,5},{5,9},{9,13},{2,6},{6,10},{10,14},{3,7},{... | collective-permute-start | bytes 165896 | tf_op jit(solution)/shard_map/ppermute | solution.py:24
  54.9 0.7 collective-permute-done
  56.2 1.3 fusion.39
  57.6 1.1 convolution_add_fusion.7
  60.1 0.5 copy-done.22
  60.6 1.2 fusion.5
  62.6 1.4 copy_add_fusion
  64.1 6.5 %scatter-add.51 = f32[1,6,6,18,256]{4,2,1,3,0:T(8,128)S(1)} dynamic-update-slice(f32[1,6,6,18,256]{4,2,1,3,0:T(8,128)S(1)} %scatter-add.50, f32[1,6,4,16,256]{4,2,1,3,0:T(4,128)S(1)} %copy_add_fusion, s32[]{:T(128)} %constant.477.clone.1, s32[]{:T(128)} %constant.477.clone.1, s32[]{:T(128)} %bitcast.22, s32[]{:T(128)} %bitcast.23, s32[]{:T(128)} %constant.477.clone.1) | dynamic-update-slice | bytes 786436 | tf_op jit(solution)/shard_map/scatter-add | solution.py:128
  70.8 2.1 add_select_fusion
  72.9 6.4 %scatter-add.54 = f32[1,6,6,18,256]{4,2,1,3,0:T(8,128)S(1)} dynamic-update-slice(f32[1,6,6,18,256]{4,2,1,3,0:T(8,128)S(1)} %scatter-add.51, f32[1,6,4,16,256]{4,2,1,3,0:T(4,128)S(1)} %add_select_fusion, s32[]{:T(128)} %constant.477.clone.1, s32[]{:T(128)} %constant.477.clone.1, s32[]{:T(128)} %bitcast.25, s32[]{:T(128)} %bitcast.26, s32[]{:T(128)} %constant.477.clone.1) | dynamic-update-slice | bytes 786436 | tf_op jit(solution)/shard_map/scatter-add | solution.py:128
  79.4 1.1 fusion.28
  80.5 0.3 slice_add_fusion.6
  80.8 5.5 %scatter-add.55 = f32[1,6,6,18,256]{4,2,1,3,0:T(8,128)S(1)} dynamic-update-slice(f32[1,6,6,18,256]{4,2,1,3,0:T(8,128)S(1)} %scatter-add.54, f32[1,6,4,16,256]{4,2,1,3,0:T(4,128)S(1)} %slice_add_fusion.6, s32[]{:T(128)} %constant.477.clone.1, s32[]{:T(128)} %constant.477.clone.1, s32[]{:T(128)} %constant.493.clone.1, s32[]{:T(128)} %constant.477.clone.1, s32[]{:T(128)} %constant.477.clone.1) | dynamic-update-slice | bytes 786436 | tf_op jit(solution)/shard_map/scatter-add | solution.py:128
  86.4 1.1 fusion.25
  87.5 0.3 slice_add_fusion.5
  87.9 5.4 %scatter-add.56 = f32[1,6,6,18,256]{4,2,1,3,0:T(8,128)S(1)} dynamic-update-slice(f32[1,6,6,18,256]{4,2,1,3,0:T(8,128)S(1)} %scatter-add.55, f32[1,6,4,16,256]{4,2,1,3,0:T(4,128)S(1)} %slice_add_fusion.5, s32[]{:T(128)} %constant.477.clone.1, s32[]{:T(128)} %constant.477.clone.1, s32[]{:T(128)} %constant.493.clone.1, s32[]{:T(128)} %constant.493.clone.1, s32[]{:T(128)} %constant.477.clone.1) | dynamic-update-slice | bytes 786436 | tf_op jit(solution)/shard_map/scatter-add | solution.py:128
  93.3 1.1 fusion.22
  94.4 0.3 slice_add_fusion.4
  94.7 5.2 %scatter-add.59 = f32[1,6,6,18,256]{4,2,1,3,0:T(8,128)S(1)} dynamic-update-slice(f32[1,6,6,18,256]{4,2,1,3,0:T(8,128)S(1)} %scatter-add.56, f32[1,6,4,16,256]{4,2,1,3,0:T(4,128)S(1)} %slice_add_fusion.4, s32[]{:T(128)} %constant.477.clone.1, s32[]{:T(128)} %constant.477.clone.1, s32[]{:T(128)} %constant.493.clone.1, s32[]{:T(128)} %constant.490.clone.1, s32[]{:T(128)} %constant.477.clone.1) | dynamic-update-slice | bytes 786436 | tf_op jit(solution)/shard_map/scatter-add | solution.py:128
  100.0 1.1 fusion.19
  101.1 0.3 slice_add_fusion.3
  101.5 5.5 %scatter-add.60 = f32[1,6,6,18,256]{4,2,1,3,0:T(8,128)S(1)} dynamic-update-slice(f32[1,6,6,18,256]{4,2,1,3,0:T(8,128)S(1)} %scatter-add.59, f32[1,6,4,16,256]{4,2,1,3,0:T(4,128)S(1)} %slice_add_fusion.3, s32[]{:T(128)} %constant.477.clone.1, s32[]{:T(128)} %constant.477.clone.1, s32[]{:T(128)} %constant.490.clone.1, s32[]{:T(128)} %constant.477.clone.1, s32[]{:T(128)} %constant.477.clone.1) | dynamic-update-slice | bytes 786436 | tf_op jit(solution)/shard_map/scatter-add | solution.py:128
  107.0 1.1 fusion.16
  108.2 0.3 slice_add_fusion.2
  108.5 5.4 %scatter-add.61 = f32[1,6,6,18,256]{4,2,1,3,0:T(8,128)S(1)} dynamic-update-slice(f32[1,6,6,18,256]{4,2,1,3,0:T(8,128)S(1)} %scatter-add.60, f32[1,6,4,16,256]{4,2,1,3,0:T(4,128)S(1)} %slice_add_fusion.2, s32[]{:T(128)} %constant.477.clone.1, s32[]{:T(128)} %constant.477.clone.1, s32[]{:T(128)} %constant.490.clone.1, s32[]{:T(128)} %constant.493.clone.1, s32[]{:T(128)} %constant.477.clone.1) | dynamic-update-slice | bytes 786436 | tf_op jit(solution)/shard_map/scatter-add | solution.py:128
  113.9 1.1 fusion.13
  115.0 0.3 slice_add_fusion.1
  115.4 5.2 %scatter-add.64 = f32[1,6,6,18,256]{4,2,1,3,0:T(8,128)S(1)} dynamic-update-slice(f32[1,6,6,18,256]{4,2,1,3,0:T(8,128)S(1)} %scatter-add.61, f32[1,6,4,16,256]{4,2,1,3,0:T(4,128)S(1)} %slice_add_fusion.1, s32[]{:T(128)} %constant.477.clone.1, s32[]{:T(128)} %constant.477.clone.1, s32[]{:T(128)} %constant.490.clone.1, s32[]{:T(128)} %constant.490.clone.1, s32[]{:T(128)} %constant.477.clone.1) | dynamic-update-slice | bytes 786436 | tf_op jit(solution)/shard_map/scatter-add | solution.py:128
  120.6 0.8 fusion.58
  121.4 0.8 broadcast_select_fusion.4
  122.3 1.2 convolution_dynamic-update-slice_fusion.8
  123.5 2.8 %collective-permute-start.2 = (f32[1,6,1,18,256]{4,2,1,3,0:T(1,128)S(1)}, f32[1,6,1,18,256]{4,2,1,3,0:T(1,128)S(1)}, u32[]{:S(2)}, u32[]{:S(2)}) collective-permute-start(f32[1,6,1,18,256]{4,2,1,3,0:T(1,128)S(1)} %get-tuple-element.226), channel_id=1, source_target_pairs={{0,4},{4,8},{8,12},{1,5},{5,9},{9,13},{2,6},{6,10},{10,14},{3,7},{... | collective-permute-start | bytes 331784 | tf_op jit(solution)/shard_map/ppermute | solution.py:24
  126.3 1.6 collective-permute-start.3
  129.9 0.9 slice.868
  130.9 3.4 %scatter-add.65 = f32[1,6,4,18,256]{4,2,1,3,0:T(4,128)} dynamic-update-slice(f32[1,6,4,18,256]{4,2,1,3,0:T(4,128)} %slice.868, f32[1,6,1,18,256]{4,2,1,3,0:T(1,128)S(1)} %slice_add_fusion.8, s32[]{:T(128)} %constant.477.clone.1, s32[]{:T(128)} %constant.477.clone.1, s32[]{:T(128)} %constant.477.clone.1, s32[]{:T(128)} %constant.477.clone.1, s32[]{:T(128)} %constant.477.clone.1) | dynamic-update-slice | bytes 221188 | tf_op jit(solution)/shard_map/scatter-add | solution.py:136
  134.3 1.2 slice_add_fusion.7
  135.6 3.4 %scatter-add.66 = f32[1,6,4,18,256]{4,2,1,3,0:T(4,128)} dynamic-update-slice(f32[1,6,4,18,256]{4,2,1,3,0:T(4,128)} %scatter-add.65, f32[1,6,1,18,256]{4,2,1,3,0:T(1,128)S(1)} %slice_add_fusion.7, s32[]{:T(128)} %constant.477.clone.1, s32[]{:T(128)} %constant.477.clone.1, s32[]{:T(128)} %constant.479.clone.1, s32[]{:T(128)} %constant.477.clone.1, s32[]{:T(128)} %constant.477.clone.1) | dynamic-update-slice | bytes 221188 | tf_op jit(solution)/shard_map/scatter-add | solution.py:137
  139.0 0.8 slice_bitcast_fusion.3
  139.9 1.2 pad_maximum_fusion.1
  141.2 0.6 convolution_bitcast_fusion
  142.0 0.8 fusion.60
  142.8 0.7 copy.147
  143.8 1.4 copy-done.1
  145.3 0.7 dynamic-slice.133
  146.6 33.7 %all-reduce.9.cloned.1.call-done = (bf16[1,6,2,16,256]{4,3,1,2,0:T(8,128)(2,1)}, bf16[1,6,2,16,256]{4,2,1,3,0:T(2,128)(2,1)}) async-done(((bf16[1,6,2,16,256]{4,3,1,2,0:T(8,128)(2,1)}, bf16[1,6,2,16,256]{4,2,1,3,0:T(2,128)(2,1)}), (bf16[1,6,2,16,256]{4,3,1,2,0:T(8,128)(2,1)}, bf16[1,6,2,16,256]{4,2,1,3,0:T(2,128)(2,1)})) %all-reduce.9.cloned.1.call-update) | async-done | bytes 196624
  180.3 1.0 convert_element_type.51
  181.3 0.8 dynamic-slice_convert_fusion
  182.3 2.8 %scatter-add.71 = f32[1,6,4,16,256]{4,2,1,3,0:T(4,128)S(1)} dynamic-update-slice(f32[1,6,4,16,256]{4,2,1,3,0:T(4,128)S(1)} %fusion.48, f32[1,6,1,16,256]{4,2,1,3,0:T(1,128)S(1)} %fusion.41, s32[]{:T(128)} %constant.477.clone.1, s32[]{:T(128)} %constant.477.clone.1, s32[]{:T(128)} %constant.477.clone.1, s32[]{:T(128)} %constant.477.clone.1, s32[]{:T(128)} %constant.477.clone.1) | dynamic-update-slice | bytes 196612 | tf_op jit(solution)/shard_map/scatter-add | solution.py:158
  185.3 2.8 %scatter-add.74 = f32[1,6,4,16,256]{4,2,1,3,0:T(4,128)S(1)} dynamic-update-slice(f32[1,6,4,16,256]{4,2,1,3,0:T(4,128)S(1)} %scatter-add.71, f32[1,6,1,16,256]{4,2,1,3,0:T(1,128)S(1)} %fusion.42, s32[]{:T(128)} %constant.477.clone.1, s32[]{:T(128)} %constant.477.clone.1, s32[]{:T(128)} %constant.479.clone.1, s32[]{:T(128)} %constant.477.clone.1, s32[]{:T(128)} %constant.477.clone.1) | dynamic-update-slice | bytes 196612 | tf_op jit(solution)/shard_map/scatter-add | solution.py:159
  188.2 0.7 copy.148
  188.9 26.6 %reduce-scatter.3.cloned.1.call-done = f32[144,256]{1,0:T(8,128)} async-done(((f32[2304,256]{1,0:T(8,128)}), f32[144,256]{1,0:T(8,128)}) %reduce-scatter.3.cloned.1.call-update) | async-done | bytes 147472 | tf_op jit(solution)/shard_map/reduce_scatter | solution.py:130
  215.5 1.6 broadcast_multiply_fusion
  (117 shorter events, 7.6 us)
Async XLA Ops:
  8.0 11.9 %copy-start.21 = (s32[5]{0:T(128)S(1)}, s32[5]{0:T(128)}, u32[]{:S(2)}) copy-start(s32[5]{0:T(128)} %constant.491.clone.1) | copy-start | bytes 64
  8.0 40.0 %all-reduce.7.cloned.1.call-start = ((), (), s32[]{:S(2)}) async-start(), calls=%async_computation.3 | async-start | bytes 393216 | tf_op jit(solution)/shard_map/psum | solution.py:13
  9.8 46.4 %all-gather.2.cloned.1.call-start = ((), (), s32[]{:S(2)}) async-start(), calls=%async_computation.1 | async-start | bytes 1253376 | tf_op jit(solution)/shard_map/all_gather | solution.py:63
  10.4 170.0 %all-reduce.9.cloned.1.call-start = ((), (), s32[]{:S(2)}) async-start(), calls=%async_computation.4 | async-start | bytes 393216
  49.3 0.9 copy-start.18
  50.3 4.5 %collective-permute-start.1 = (bf16[1,6,1,18,256]{4,3,2,1,0:T(8,128)(2,1)S(1)}, bf16[1,6,1,18,256]{4,3,2,1,0:T(8,128)(2,1)S(1)}, u32[]{:S(2)}, u32[]{:S(2)}) collective-permute-start(bf16[1,6,1,18,256]{4,3,2,1,0:T(8,128)(2,1)S(1)} %get-tuple-element.241), channel_id=1, source_target_pairs={{4,0},{8,4},{12,8},{5,1},{9,5},{13,9},{6,2},{10,6},{14,10},{7,3},{... | collective-permute-start | bytes 165896 | tf_op jit(solution)/shard_map/ppermute | solution.py:26
  51.6 3.9 %collective-permute-start = (bf16[1,6,1,18,256]{4,3,2,1,0:T(8,128)(2,1)S(1)}, bf16[1,6,1,18,256]{4,3,2,1,0:T(8,128)(2,1)S(1)}, u32[]{:S(2)}, u32[]{:S(2)}) collective-permute-start(bf16[1,6,1,18,256]{4,3,2,1,0:T(8,128)(2,1)S(1)} %get-tuple-element.240), channel_id=1, source_target_pairs={{0,4},{4,8},{8,12},{1,5},{5,9},{9,13},{2,6},{6,10},{10,14},{3,7},{... | collective-permute-start | bytes 165896 | tf_op jit(solution)/shard_map/ppermute | solution.py:24
  56.1 2.8 %copy-start.3 = (bf16[1,6,4,16,256]{4,3,2,1,0:T(8,128)(2,1)}, bf16[1,6,4,16,256]{4,3,2,1,0:T(8,128)(2,1)S(1)}, u32[]{:S(2)}) copy-start(bf16[1,6,4,16,256]{4,3,2,1,0:T(8,128)(2,1)S(1)} %get-tuple-element.237) | copy-start | bytes 589828
  56.1 2.8 %copy-start.14 = (bf16[1,6,4,16,256]{4,3,2,1,0:T(8,128)(2,1)}, bf16[1,6,4,16,256]{4,3,2,1,0:T(8,128)(2,1)S(1)}, u32[]{:S(2)}) copy-start(bf16[1,6,4,16,256]{4,3,2,1,0:T(8,128)(2,1)S(1)} %get-tuple-element.235) | copy-start | bytes 589828
  56.1 2.8 %copy-start.16 = (bf16[1,6,4,16,256]{4,3,2,1,0:T(8,128)(2,1)}, bf16[1,6,4,16,256]{4,3,2,1,0:T(8,128)(2,1)S(1)}, u32[]{:S(2)}) copy-start(bf16[1,6,4,16,256]{4,3,2,1,0:T(8,128)(2,1)S(1)} %get-tuple-element.236) | copy-start | bytes 589828
  56.1 2.8 %copy-start.12 = (bf16[1,6,4,16,256]{4,3,2,1,0:T(8,128)(2,1)}, bf16[1,6,4,16,256]{4,3,2,1,0:T(8,128)(2,1)S(1)}, u32[]{:S(2)}) copy-start(bf16[1,6,4,16,256]{4,3,2,1,0:T(8,128)(2,1)S(1)} %get-tuple-element.234) | copy-start | bytes 589828
  56.1 3.0 %copy-start.10 = (bf16[1,6,4,16,256]{4,3,2,1,0:T(8,128)(2,1)}, bf16[1,6,4,16,256]{4,3,2,1,0:T(8,128)(2,1)S(1)}, u32[]{:S(2)}) copy-start(bf16[1,6,4,16,256]{4,3,2,1,0:T(8,128)(2,1)S(1)} %get-tuple-element.233) | copy-start | bytes 589828
  56.2 3.3 %copy-start.8 = (bf16[1,6,4,16,256]{4,3,2,1,0:T(8,128)(2,1)}, bf16[1,6,4,16,256]{4,3,2,1,0:T(8,128)(2,1)S(1)}, u32[]{:S(2)}) copy-start(bf16[1,6,4,16,256]{4,3,2,1,0:T(8,128)(2,1)S(1)} %get-tuple-element.232) | copy-start | bytes 589828
  56.2 3.5 %copy-start.6 = (bf16[1,6,4,16,256]{4,3,2,1,0:T(8,128)(2,1)}, bf16[1,6,4,16,256]{4,3,2,1,0:T(8,128)(2,1)S(1)}, u32[]{:S(2)}) copy-start(bf16[1,6,4,16,256]{4,3,2,1,0:T(8,128)(2,1)S(1)} %get-tuple-element.231) | copy-start | bytes 589828
  56.2 3.7 %copy-start.4 = (bf16[1,6,4,16,256]{4,3,2,1,0:T(8,128)(2,1)}, bf16[1,6,4,16,256]{4,3,2,1,0:T(8,128)(2,1)S(1)}, u32[]{:S(2)}) copy-start(bf16[1,6,4,16,256]{4,3,2,1,0:T(8,128)(2,1)S(1)} %get-tuple-element.230) | copy-start | bytes 589828
  56.2 3.9 %copy-start.19 = (bf16[1,6,4,16,256]{4,3,2,1,0:T(8,128)(2,1)}, bf16[1,6,4,16,256]{4,3,2,1,0:T(8,128)(2,1)S(1)}, u32[]{:S(2)}) copy-start(bf16[1,6,4,16,256]{4,3,2,1,0:T(8,128)(2,1)S(1)} %get-tuple-element.229) | copy-start | bytes 589828
  56.2 2.5 %copy-start = (bf16[2304,256]{1,0:T(8,128)(2,1)S(1)}, bf16[2304,256]{1,0:T(8,128)(2,1)}, u32[]{:S(2)}) copy-start(bf16[2304,256]{1,0:T(8,128)(2,1)} %all-gather.2.cloned.1.call-done) | copy-start | bytes 3538948
  59.6 0.9 copy-start.22
  120.6 7.3 %copy-start.17 = (bf16[1,6,4,16,256]{4,3,2,1,0:T(8,128)(2,1)S(1)}, bf16[1,6,4,16,256]{4,3,2,1,0:T(8,128)(2,1)}, u32[]{:S(2)}) copy-start(bf16[1,6,4,16,256]{4,3,2,1,0:T(8,128)(2,1)} %copy-done.16) | copy-start | bytes 589828
  120.6 7.6 %copy-start.15 = (bf16[1,6,4,16,256]{4,3,2,1,0:T(8,128)(2,1)S(1)}, bf16[1,6,4,16,256]{4,3,2,1,0:T(8,128)(2,1)}, u32[]{:S(2)}) copy-start(bf16[1,6,4,16,256]{4,3,2,1,0:T(8,128)(2,1)} %copy-done.14) | copy-start | bytes 589828
  121.4 7.0 %copy-start.13 = (bf16[1,6,4,16,256]{4,3,2,1,0:T(8,128)(2,1)S(1)}, bf16[1,6,4,16,256]{4,3,2,1,0:T(8,128)(2,1)}, u32[]{:S(2)}) copy-start(bf16[1,6,4,16,256]{4,3,2,1,0:T(8,128)(2,1)} %copy-done.12) | copy-start | bytes 589828
  122.3 6.5 %copy-start.11 = (bf16[1,6,4,16,256]{4,3,2,1,0:T(8,128)(2,1)S(1)}, bf16[1,6,4,16,256]{4,3,2,1,0:T(8,128)(2,1)}, u32[]{:S(2)}) copy-start(bf16[1,6,4,16,256]{4,3,2,1,0:T(8,128)(2,1)} %copy-done.10) | copy-start | bytes 589828
  123.5 7.2 %collective-permute-start.2 = (f32[1,6,1,18,256]{4,2,1,3,0:T(1,128)S(1)}, f32[1,6,1,18,256]{4,2,1,3,0:T(1,128)S(1)}, u32[]{:S(2)}, u32[]{:S(2)}) collective-permute-start(f32[1,6,1,18,256]{4,2,1,3,0:T(1,128)S(1)} %get-tuple-element.226), channel_id=1, source_target_pairs={{0,4},{4,8},{8,12},{1,5},{5,9},{9,13},{2,6},{6,10},{10,14},{3,7},{... | collective-permute-start | bytes 331784 | tf_op jit(solution)/shard_map/ppermute | solution.py:24
  126.3 2.8 %copy-start.9 = (bf16[1,6,4,16,256]{4,3,2,1,0:T(8,128)(2,1)S(1)}, bf16[1,6,4,16,256]{4,3,2,1,0:T(8,128)(2,1)}, u32[]{:S(2)}) copy-start(bf16[1,6,4,16,256]{4,3,2,1,0:T(8,128)(2,1)} %copy-done.8) | copy-start | bytes 589828
  126.3 8.0 %collective-permute-start.3 = (f32[1,6,1,18,256]{4,2,1,3,0:T(1,128)}, f32[1,6,1,18,256]{4,2,1,3,0:T(1,128)}, u32[]{:S(2)}, u32[]{:S(2)}) collective-permute-start(f32[1,6,1,18,256]{4,2,1,3,0:T(1,128)} %get-tuple-element.225), channel_id=1, source_target_pairs={{4,0},{8,4},{12,8},{5,1},{9,5},{13,9},{6,2},{10,6},{14,10},{7,3},{... | collective-permute-start | bytes 331784 | tf_op jit(solution)/shard_map/ppermute | solution.py:26
  128.2 1.1 copy-start.7
  128.5 1.1 copy-start.5
  141.9 1.6 copy-start.20
  143.4 72.0 %reduce-scatter.3.cloned.1.call-start = ((), (), s32[]{:S(2)}) async-start(), calls=%async_computation.2 | async-start | bytes 2506752 | tf_op jit(solution)/shard_map/reduce_scatter | solution.py:130
  143.8 1.4 copy-start.1
  143.8 1.5 copy-start.23
  143.8 2.8 %copy-start.2 = (f32[1,6,4,18,256]{4,2,1,3,0:T(4,128)S(1)}, f32[1,6,4,18,256]{4,2,1,3,0:T(4,128)}, u32[]{:S(2)}) copy-start(f32[1,6,4,18,256]{4,2,1,3,0:T(4,128)} %scatter-add.66) | copy-start | bytes 1327108
Sparse Core Ops, SparseCore 0:
  11.8 36.2 all-reduce.6
  143.6 36.7 all-reduce.8
Sparse Core Ops, SparseCore 1:
  12.8 41.2 all-gather.1
  147.7 67.7 reduce-scatter.2
where the time goes:
time: 225 us; the launch traced here: 224 us
  waiting for transfers between devices  89 us (40%)
  local copies, waits for them, and re-layouts  69.7 us (31%)
  between operations  17.2 us (8%)
  other arithmetic  16.9 us (8%)
  matrix products  16.6 us (7%)
  starting transfers between devices  8.86 us (4%)
  blocking collectives  6.29 us (3%)
    scatter-add x9, local copies, waits for them, and re-layouts, shards(): grad_pad = grad_pad.at[:, :, row_step:row_step + band_rows, col_step:col_...  45.4 us
    unnamed x5, waiting for transfers between devices  34.3 us
    psum x1, waiting for transfers between devices, from_root(): return lax.psum(kept, axis)  27.5 us
    reduce_scatter x1, waiting for transfers between devices, shards(): lax.psum_scatter(local_grad, ('tile', 'member'), scatter_dimension=0, til...  26.6 us
    dot_general x9, matrix products, shards(): jnp.dot(act_grad, kernel_rows.T, preferred_element_type=jnp.float32)  7.52 us
    all_gather x1, blocking collectives, shards(): all_columns = lax.all_gather(side_columns, 'tile', axis=3, tiled=True)  6.29 us
    ppermute x2, starting transfers between devices, extended(): lax.ppermute(tail, axis, [(i, (i + 1) % count) for i in range(ends)])  5.79 us
    dot_general x9, matrix products, shards(): jnp.dot(window, full_weight[offset * channels:(offset + 1) * channels], p...  4.9 us
  transfers between devices with their start and end apart: 8, of which 4 were waited for; matrix products, arithmetic and copies ran while one was open for 10% of the time, Pallas kernels for 0%

commit v1 on v0

--- a/solution.py
+++ b/solution.py
@@ -1,8 +1,12 @@
+import functools
 import math
 
 import jax
 import jax.numpy as jnp
+import numpy as np
 from jax import lax
+from jax.experimental import pallas as pl
+from jax.experimental.pallas import tpu as pltpu
 from jax.sharding import PartitionSpec as P
 
 gelu_scale = 0.7978845608028654
@@ -52,7 +56,7 @@
     return line_grad.reshape(members, face_count, 4, face_size, channels)
 
 
-def shards(fields, weight, cotangent, adjacency):
+def plain_shards(fields, weight, cotangent, adjacency):
     members, face_count, band_rows, face_size, channels = fields.shape
     position = lax.axis_index("tile")
     tile_count = lax.axis_size("tile")
@@ -161,6 +165,391 @@
     return (activation, input_grad, weight_grad)
 
 
+MESH = pl.DeviceIdType.MESH
+COPIES = 30
+WZ, WX, WS, WD, EX, GX, R1, X2, Z3 = 0, 3, 7, 11, 15, 18, 21, 23, 27
+
+
+def one_hot(index_column, width):
+    rows = index_column.shape[0]
+    lanes = lax.broadcasted_iota(jnp.int32, (rows, width), 1)
+    return jnp.where(index_column == lanes, 1.0, 0.0)
+
+
+def fused_kernel(
+    dims,
+    scale,
+    fields_ref,
+    weight_ref,
+    cot_ref,
+    pad_index_ref,
+    cell_index_ref,
+    act_ref,
+    in_grad_ref,
+    w_grad_ref,
+    full_w,
+    edges,
+    grad_edges,
+    pick,
+    padded,
+    shifted,
+    total,
+    outgoing,
+    from_core,
+    to_x,
+    from_x,
+    to_z,
+    from_z,
+    send_sem,
+    recv_sem,
+):
+    faces, band, size, channels = dims
+    cells = faces * band * size
+    line = faces * size
+    side = faces * 2 * band
+    block = weight_ref.shape[0]
+    quarter = 4 * block
+    f32, bf16 = jnp.float32, jnp.bfloat16
+    me = lax.axis_index("tile")
+    z = lax.axis_index("member")
+    chip, core = me // 2, me % 2
+    sib = chip * 2 + (1 - core)
+    across = (1 - chip) * 2 + core
+    diag = (1 - chip) * 2 + (1 - core)
+    tile_peers = (sib, across, diag)
+
+    def remote(src, dst, sem, target):
+        return pltpu.make_async_remote_copy(
+            src_ref=src,
+            dst_ref=dst,
+            send_sem=send_sem.at[sem],
+            recv_sem=recv_sem.at[sem],
+            device_id=target,
+            device_id_type=MESH,
+        )
+
+    def tile_id(t):
+        return {"tile": t}
+
+    def member_id(k):
+        return {"member": (z + k) % 4}
+
+    def w_block(t, m):
+        return full_w.at[pl.ds(pl.multiple_of((t * 4 + m) * block, 16), block)]
+
+    barrier = pltpu.get_barrier_semaphore()
+    for t in tile_peers:
+        pl.semaphore_signal(barrier, inc=1, device_id=tile_id(t), device_id_type=MESH)
+    for k in range(1, 4):
+        pl.semaphore_signal(barrier, inc=1, device_id=member_id(k), device_id_type=MESH)
+
+    side_pick = one_hot(cell_index_ref[0:side, 5:6], cells).astype(bf16)
+
+    def own_edges(values, out):
+        cube = values.reshape(faces, band, size, channels)
+        out[me, 0:side] = jnp.dot(side_pick, values, preferred_element_type=f32).astype(bf16)
+        out[me, side : side + line] = cube[:, 0].reshape(line, channels)
+        out[me, side + line : side + 2 * line] = cube[:, band - 1].reshape(line, channels)
+
+    w_block(me, z)[...] = weight_ref[...]
+    own_edges(fields_ref[...], edges)
+    pl.semaphore_wait(barrier, 6)
+
+    started = []
+
+    def go(copy):
+        copy.start()
+        started.append(copy)
+
+    for k in (2, 1, 3):
+        go(remote(w_block(me, z), w_block(me, z), WZ + k - 1, member_id(k)))
+    for k, t in enumerate(tile_peers):
+        go(remote(edges.at[me], edges.at[me], EX + k, tile_id(t)))
+
+    def w_spread(k):
+        part = w_block(me, (z + 4 - k) % 4)
+        if k:
+            remote(part, part, WZ + k - 1, member_id(k)).wait_recv()
+        go(remote(part, part, WX + k, tile_id(across)))
+        go(remote(part, part, WS + k, tile_id(sib)))
+
+    w_spread(0)
+    for dx in range(3):
+        pick[dx] = one_hot(pad_index_ref[:, dx : dx + 1], 4 * side + 2 * line).astype(bf16)
+    for k in (1, 3, 2):
+        w_spread(k)
+
+    def columns(rows):
+        return lax.broadcasted_iota(jnp.int32, (rows, 1), 0) % size
+
+    def moved(values, step):
+        rows = values.shape[0]
+        if step == 0:
+            return values
+        if step < 0:
+            return jnp.where(columns(rows) == 0, 0.0, pltpu.roll(values, 1, 0))
+        return jnp.where(columns(rows) == size - 1, 0.0, pltpu.roll(values, rows - 1, 0))
+
+    def with_halo(values, buf):
+        above = buf[jnp.maximum(me - 1, 0), side + line : side + 2 * line].astype(f32)
+        below = buf[jnp.minimum(me + 1, 3), side : side + line].astype(f32)
+        above = jnp.where(me > 0, above, 0.0).reshape(faces, 1, size, channels)
+        below = jnp.where(me < 3, below, 0.0).reshape(faces, 1, size, channels)
+        own = values.astype(f32).reshape(faces, band, size, channels)
+        return jnp.concatenate([above, own, below], axis=1).reshape(-1, channels)
+
+    def lines_of(buf):
+        return jnp.concatenate(
+            [buf[t, 0:side] for t in range(4)]
+            + [buf[0, side : side + line], buf[3, side + line : side + 2 * line]],
+            axis=0,
+        )
+
+    for k, t in enumerate(tile_peers):
+        remote(edges.at[t], edges.at[t], EX + k, tile_id(t)).wait_recv()
+    lines = lines_of(edges)
+    center = with_halo(fields_ref[...], edges)
+    for dx in range(3):
+        values = moved(center, dx - 1) + jnp.dot(pick[dx], lines, preferred_element_type=f32)
+        padded[dx] = values.astype(bf16).reshape(faces, band + 2, size, channels)
+
+    for k in (0, 1, 3, 2):
+        part = w_block(across, (z + 4 - k) % 4)
+        remote(part, part, WX + k, tile_id(across)).wait_recv()
+        go(remote(part, part, WD + k, tile_id(sib)))
+    for k in range(4):
+        part = w_block(sib, (z + 4 - k) % 4)
+        remote(part, part, WS + k, tile_id(sib)).wait_recv()
+        part = w_block(diag, (z + 4 - k) % 4)
+        remote(part, part, WD + k, tile_id(sib)).wait_recv()
+
+    def window(dy, dx):
+        return padded[dx, :, dy : dy + band].reshape(cells, channels)
+
+    def w_of(dy, dx):
+        first = (3 * dy + dx) * channels
+        return full_w[first : first + channels]
+
+    pre = jnp.zeros((cells, channels), f32)
+    for dy in range(3):
+        for dx in range(3):
+            pre = pre + jnp.dot(window(dy, dx), w_of(dy, dx), preferred_element_type=f32)
+    square = pre * pre
+    bend = jnp.tanh(gelu_scale * (pre + 0.044715 * pre * square))
+    act_ref[...] = (0.5 * pre * (1.0 + bend)).astype(bf16)
+    slope = 0.5 * (1.0 + bend) + 0.5 * pre * (1.0 - bend * bend) * (
+        gelu_scale * (1.0 + 3 * 0.044715 * square)
+    )
+    act_grad = (cot_ref[...].astype(f32) * slope).astype(bf16)
+    own_edges(act_grad, grad_edges)
+    for k, t in enumerate(tile_peers):
+        go(remote(grad_edges.at[me], grad_edges.at[me], GX + k, tile_id(t)))
+
+    for dy in range(3):
+        for dx in range(3):
+            first = (3 * dy + dx) * channels
+            part = lax.dot_general(
+                window(dy, dx), act_grad, (((0,), (0,)), ((), ())), preferred_element_type=f32
+            )
+            total[first : first + channels] = part
+            outgoing[first : first + channels] = part.astype(bf16)
+
+    def quarter_at(t):
+        return pl.ds(pl.multiple_of(t * quarter, 16), quarter)
+
+    def part_at(m):
+        return pl.ds(pl.multiple_of(m * block, 16), block)
+
+    def row_at(t, m):
+        return pl.ds(pl.multiple_of((t * 4 + m) * block, 16), block)
+
+    go(remote(outgoing.at[quarter_at(diag)], from_core.at[0], R1, tile_id(sib)))
+    go(remote(outgoing.at[quarter_at(sib)], from_core.at[1], R1 + 1, tile_id(sib)))
+
+    remote(from_core.at[0], from_core.at[0], R1, tile_id(sib)).wait_recv()
+    for k in (2, 1, 3, 0):
+        m = (z + k) % 4
+        to_x[part_at(m)] = (
+            total[row_at(across, m)] + from_core[0, part_at(m)].astype(f32)
+        ).astype(bf16)
+        go(remote(to_x.at[part_at(m)], from_x.at[part_at(m)], X2 + k, tile_id(across)))
+
+    for k, t in enumerate(tile_peers):
+        remote(grad_edges.at[t], grad_edges.at[t], GX + k, tile_id(t)).wait_recv()
+    center = with_halo(act_grad, grad_edges)
+    for dx in range(3):
+        shifted[dx] = (
+            moved(center, 1 - dx).astype(bf16).reshape(faces, band + 2, size, channels)
+        )
+    grad = jnp.zeros((cells, channels), f32)
+    over_outputs = (((1,), (1,)), ((), ()))
+    for dy in range(3):
+        for dx in range(3):
+            grad = grad + lax.dot_general(
+                shifted[dx, :, 2 - dy : 2 - dy + band].reshape(cells, channels),
+                w_of(dy, dx),
+                over_outputs,
+                preferred_element_type=f32,
+            )
+
+    remote(from_core.at[1], from_core.at[1], R1 + 1, tile_id(sib)).wait_recv()
+    for k in (2, 1, 3, 0):
+        m = (z + k) % 4
+        remote(to_x.at[part_at(m)], from_x.at[part_at(m)], X2 + k, tile_id(across)).wait_recv()
+        mine = (
+            total[row_at(me, m)]
+            + from_core[1, part_at(m)].astype(f32)
+            + from_x[part_at(m)].astype(f32)
+        )
+        if k:
+            to_z[k - 1] = mine.astype(bf16)
+            go(remote(to_z.at[k - 1], from_z.at[k - 1], Z3 + k - 1, member_id(k)))
+        else:
+            w_grad_ref[...] = mine
+
+    lines = lines_of(grad_edges)
+    taps = [
+        jnp.dot(
+            one_hot(cell_index_ref[:, 2 + s : 3 + s], 4 * side + 2 * line).astype(bf16),
+            lines,
+            preferred_element_type=f32,
+        ).astype(bf16)
+        for s in range(3)
+    ]
+    pieces = []
+    for edge in range(4):
+        piece = jnp.zeros((line, channels), f32)
+        for s in range(3):
+            dy, dx = ((0, s), (2, s), (s, 0), (s, 2))[edge]
+            piece = piece + lax.dot_general(
+                taps[s][edge * line : (edge + 1) * line],
+                w_of(dy, dx),
+                over_outputs,
+                preferred_element_type=f32,
+            )
+        pieces.append(piece)
+    cycle = jnp.concatenate(pieces, axis=0)
+    route = (
+        one_hot(cell_index_ref[:, 0:1], 4 * line) + one_hot(cell_index_ref[:, 1:2], 4 * line)
+    ).astype(bf16)
+    high = cycle.astype(bf16)
+    low = (cycle - high.astype(f32)).astype(bf16)
+    grad = grad + jnp.dot(route, high, preferred_element_type=f32)
+    grad = grad + jnp.dot(route, low, preferred_element_type=f32)
+    in_grad_ref[...] = grad.astype(bf16)
+
+    result = w_grad_ref[...]
+    for k in range(1, 4):
+        remote(from_z.at[k - 1], from_z.at[k - 1], Z3 + k - 1, member_id(k)).wait_recv()
+        result = result + from_z[k - 1].astype(f32)
+    w_grad_ref[...] = result * scale
+    for copy in started:
+        copy.wait_send()
+
+
+def index_tables(adjacency, faces, band, size):
+    position = lax.axis_index("tile")
+    face, edge, flag = (adjacency[:, :, i][:, :, None] for i in range(3))
+    along = jnp.arange(size, dtype=jnp.int32)[None, None, :]
+    u = jnp.where(flag == 1, size - 1 - along, along)
+    side, line = faces * 2 * band, faces * size
+    on_rows = 4 * side + edge * line + face * size + u
+    on_sides = (u // band) * side + face * 2 * band + (edge - 2) * band + u % band
+    source = jnp.where(edge < 2, on_rows, on_sides)
+    cycle = edge * line + face * size + u
+
+    def framed(values, inner):
+        middle = jnp.full((faces, size, inner), -1, jnp.int32)
+        return jnp.concatenate([values[:, 2][:, :, None], middle, values[:, 3][:, :, None]], axis=2)
+
+    def ended(values):
+        return jnp.pad(values, ((0, 0), (1, 1)), constant_values=-1)[:, None]
+
+    whole = jnp.concatenate([ended(source[:, 0]), framed(source, size), ended(source[:, 1])], axis=1)
+    rows = lax.dynamic_slice_in_dim(whole, position * band, band + 2, 1)
+    pad_index = jnp.stack([rows[:, :, dx : dx + size] for dx in range(3)], axis=-1).reshape(-1, 3)
+    by_column = framed(cycle, size - 2)
+    by_row = jnp.concatenate(
+        [
+            cycle[:, 0][:, None],
+            jnp.full((faces, size - 2, size), -1, jnp.int32),
+            cycle[:, 1][:, None],
+        ],
+        axis=1,
+    )
+    both = jnp.stack([by_column, by_row], axis=-1)
+    both = lax.dynamic_slice_in_dim(both, position * band, band, 1).reshape(-1, 2)
+
+    e, f, t = np.meshgrid(np.arange(4), np.arange(faces), np.arange(size), indexing="ij")
+    fixed = np.full((faces * band * size, 4), -1, np.int32)
+    for s in range(3):
+        v = t + 1 - s
+        at = np.where(
+            e < 2,
+            4 * side + e * line + f * size + v,
+            (v // band) * side + f * 2 * band + (e - 2) * band + v % band,
+        )
+        fixed[:, s] = np.where((v < 0) | (v >= size), -1, at).reshape(-1)
+    f, k, r = np.meshgrid(np.arange(faces), np.arange(2), np.arange(band), indexing="ij")
+    fixed[:side, 3] = (f * band * size + r * size + k * (size - 1)).reshape(-1)
+    cell_index = jnp.concatenate([both, jnp.asarray(fixed)], axis=1)
+    return pad_index, cell_index
+
+
+def shards(fields, weight, cotangent, adjacency):
+    members, faces, band, size, channels = fields.shape
+    tiles, across = lax.axis_size("tile"), lax.axis_size("member")
+    block = weight.shape[0]
+    fits = tiles == 4 and across == 4 and members == 1 and band * tiles == size
+    if not (fits and size == 16 and block % 16 == 0 and (faces * 2 * band) % 16 == 0):
+        return plain_shards(fields, weight, cotangent, adjacency)
+    cells = faces * band * size
+    pad_index, cell_index = index_tables(adjacency, faces, band, size)
+    side, line = faces * 2 * band, faces * size
+    bf16, f32 = jnp.bfloat16, jnp.float32
+    scale = 1.0 / math.sqrt(cells * tiles * across)
+    rows = block * tiles * across
+    whole = pl.BlockSpec(memory_space=pltpu.VMEM)
+    lines = 4 * side + 2 * line
+    act, in_grad, w_grad = pl.pallas_call(
+        functools.partial(fused_kernel, (faces, band, size, channels), scale),
+        out_shape=(
+            jax.ShapeDtypeStruct((cells, channels), bf16),
+            jax.ShapeDtypeStruct((cells, channels), bf16),
+            jax.ShapeDtypeStruct((block, channels), f32),
+        ),
+        in_specs=[whole] * 5,
+        out_specs=(whole,) * 3,
+        scratch_shapes=[
+            pltpu.VMEM((rows, channels), bf16),
+            pltpu.VMEM((4, side + 2 * line, channels), bf16),
+            pltpu.VMEM((4, side + 2 * line, channels), bf16),
+            pltpu.VMEM((3, faces * (band + 2) * size, lines), bf16),
+            pltpu.VMEM((3, faces, band + 2, size, channels), bf16),
+            pltpu.VMEM((3, faces, band + 2, size, channels), bf16),
+            pltpu.VMEM((rows, channels), f32),
+            pltpu.VMEM((rows, channels), bf16),
+            pltpu.VMEM((2, 4 * block, channels), bf16),
+            pltpu.VMEM((4 * block, channels), bf16),
+            pltpu.VMEM((4 * block, channels), bf16),
+            pltpu.VMEM((3, block, channels), bf16),
+            pltpu.VMEM((3, block, channels), bf16),
+            pltpu.SemaphoreType.DMA((COPIES,)),
+            pltpu.SemaphoreType.DMA((COPIES,)),
+        ],
+        compiler_params=pltpu.CompilerParams(
+            collective_id=0, has_side_effects=True, vmem_limit_bytes=40 * 1024 * 1024
+        ),
+    )(
+        fields.reshape(cells, channels),
+        weight,
+        cotangent.reshape(cells, channels),
+        pad_index,
+        cell_index,
+    )
+    return act.reshape(fields.shape), in_grad.reshape(fields.shape), w_grad
+
+
 def solution(mesh):
     in_specs = (
         P(("groups", "member"), None, "tile", None, None),

time: 225 us -> 45 us (0.20)
  waiting for transfers between devices: 89 us -> 0 us
  local copies, waits for them, and re-layouts: 69.7 us -> 5.38 us
  Pallas kernels: 0 us -> 38.3 us
  matrix products: 16.6 us -> 0 us
  other arithmetic: 16.9 us -> 0.34 us
  between operations: 17.2 us -> 0.76 us
  starting transfers between devices: 8.86 us -> 0 us
  blocking collectives: 6.29 us -> 0 us
    scatter-add x13 -> x0, local copies, waits for them, and re-layouts: 57.7 us -> none  [the longest x9 45.4 us: shards(): grad_pad = grad_pad.at[:, :, row_step:row_step + band_rows, col_step:col_...]
    pallas_call x0 -> x1, Pallas kernels: none -> 38.3 us  [shards(): pl.pallas_call(functools.partial(fused_kernel, (faces, band, size, channe...]
    unnamed x5 -> x0, waiting for transfers between devices: 34.3 us -> none
    psum x1 -> x0, waiting for transfers between devices: 27.5 us -> none  [from_root(): return lax.psum(kept, axis)]
    reduce_scatter x1 -> x0, waiting for transfers between devices: 26.6 us -> none  [shards(): lax.psum_scatter(local_grad, ('tile', 'member'), scatter_dimension=0, til...]
    dot_general x29 -> x0, matrix products: 16.6 us -> none  [the longest x9 7.52 us: shards(): jnp.dot(act_grad, kernel_rows.T, preferred_element_type=jnp.float32)]
    ppermute x4 -> x0, starting transfers between devices: 8.69 us -> none  [the longest x2 5.79 us: extended(): lax.ppermute(tail, axis, [(i, (i + 1) % count) for i in range(ends)])]
    all_gather x1 -> x0, blocking collectives: 6.29 us -> none  [shards(): all_columns = lax.all_gather(side_columns, 'tile', axis=3, tiled=True)]
  transfers between devices with their start and end apart: 8 -> 0, of which waited for: 4 -> 0; matrix products, arithmetic and copies ran while one was open for 10% -> 0% of each run, Pallas kernels for 0% -> 0%
where the time goes in v1:
time: 45 us; the launch traced here: 44.8 us
  Pallas kernels  38.3 us (85%)
  local copies, waits for them, and re-layouts  5.38 us (12%)
  between operations  0.76 us (2%)
    pallas_call x1, Pallas kernels, shards(): pl.pallas_call(functools.partial(fused_kernel, (faces, band, size, channe...  38.3 us
    unnamed x13, local copies, waits for them, and re-layouts  4.04 us

profile of v1, /device:TPU:0, one launch (start us, length us, event | category | flops | bytes accessed | tf_op | source)
XLA Modules:
  0.0 44.8 jit_solution(11126677413331446910)
XLA Ops:
  0.6 0.0 copy-start.3
  0.7 0.1 pad.17.clone
  0.7 0.6 %copy-done.3 = s32[6,4,3]{0,1,2:T(4,128)S(1)} copy-done((s32[6,4,3]{0,1,2:T(4,128)S(1)}, s32[6,4,3]{0,1,2:T(4,128)}, u32[]{:S(2)}) %copy-start.3) | copy-done | bytes 312
  1.3 0.1 pad_dynamic-slice_fusion.6
  1.4 0.1 fusion.12
  1.5 0.1 pad_bitcast_fusion
  1.6 0.1 pad_bitcast_fusion.1
  1.7 0.1 broadcast_in_dim_squeeze.17
  1.8 0.1 broadcast_in_dim_squeeze.16
  1.9 0.1 fusion.1
  2.0 0.1 broadcast_in_dim_squeeze.18
  2.0 0.1 broadcast_in_dim_squeeze.19
  2.1 0.1 add_bitcast_fusion.1
  2.2 0.0 copy-start.4
  2.2 0.1 reshape.35
  2.3 0.6 %copy-done.4 = s32[384,4]{0,1:T(4,128)S(1)} copy-done((s32[384,4]{0,1:T(4,128)S(1)}, s32[384,4]{0,1:T(4,128)}, u32[]{:S(2)}) %copy-start.4) | copy-done | bytes 6168
  2.9 0.1 fusion.17
  3.0 0.1 stack.21
  3.1 0.1 stack.22
  3.2 0.1 stack.23
  3.3 0.0 copy-start.1
  3.3 0.1 copy.37.cell_index_ref
  3.4 0.0 copy-start
  3.5 0.0 copy-start.2
  3.5 0.2 copy.36.pad_index_ref
  3.6 0.6 %copy-done.1 = bf16[1,6,4,16,256]{4,3,2,1,0:T(8,128)(2,1)S(1)} copy-done((bf16[1,6,4,16,256]{4,3,2,1,0:T(8,128)(2,1)S(1)}, bf16[1,6,4,16,256]{4,3,2,1,0:T(8,128)(2,1)}, u32[]{:S(2)}) %copy-start.1) | copy-done | bytes 196632
  4.2 0.2 copy-done
  4.4 0.1 copy-done.2
  4.5 38.3 %shard_map.76 = (bf16[384,256]{1,0:T(8,128)(2,1)S(1)}, bf16[384,256]{1,0:T(8,128)(2,1)S(1)}, f32[144,256]{1,0:T(8,128)S(1)}) custom-call(bf16[384,256]{1,0:T(8,128)(2,1)S(1)} %bitcast.40, bf16[144,256]{1,0:T(8,128)(2,1)S(1)} %copy-done.2, bf16[384,256]{1,0:T(8,128)(2,1)S(1)} %bitcast.41, s32[576,3]{1,0:T(8,128)S(1)} %copy.36.pad_index_ref, ...), custom_call_target="tpu_custom_call" | custom-call | tf_op jit(solution)/shard_map/pallas_call | solution.py:514
  42.7 0.7 %copy.41 = bf16[1,6,4,16,256]{4,3,2,1,0:T(8,128)(2,1)} copy(bf16[1,6,4,16,256]{4,3,2,1,0:T(8,128)(2,1)S(1)} %bitcast.39) | data formatting | bytes 393216
  43.4 0.7 %copy.42 = bf16[1,6,4,16,256]{4,3,2,1,0:T(8,128)(2,1)} copy(bf16[1,6,4,16,256]{4,3,2,1,0:T(8,128)(2,1)S(1)} %bitcast.38) | data formatting | bytes 393216
  44.1 0.7 %copy.43 = f32[144,256]{1,0:T(8,128)} copy(f32[144,256]{1,0:T(8,128)S(1)} %get-tuple-element.39) | data formatting | bytes 294912
  (13 shorter events, 0.1 us)
Async XLA Ops:
  0.6 0.7 %copy-start.3 = (s32[6,4,3]{0,1,2:T(4,128)S(1)}, s32[6,4,3]{0,1,2:T(4,128)}, u32[]{:S(2)}) copy-start(s32[6,4,3]{0,1,2:T(4,128)} %param.8) | copy-start | bytes 868
  2.2 0.7 %copy-start.4 = (s32[384,4]{0,1:T(4,128)S(1)}, s32[384,4]{0,1:T(4,128)}, u32[]{:S(2)}) copy-start(s32[384,4]{0,1:T(4,128)} %constant.60.clone) | copy-start | bytes 18436
  3.3 0.9 %copy-start.1 = (bf16[1,6,4,16,256]{4,3,2,1,0:T(8,128)(2,1)S(1)}, bf16[1,6,4,16,256]{4,3,2,1,0:T(8,128)(2,1)}, u32[]{:S(2)}) copy-start(bf16[1,6,4,16,256]{4,3,2,1,0:T(8,128)(2,1)} %param.7) | copy-start | bytes 589828
  3.4 1.0 %copy-start = (bf16[1,6,4,16,256]{4,3,2,1,0:T(8,128)(2,1)S(1)}, bf16[1,6,4,16,256]{4,3,2,1,0:T(8,128)(2,1)}, u32[]{:S(2)}) copy-start(bf16[1,6,4,16,256]{4,3,2,1,0:T(8,128)(2,1)} %param.5) | copy-start | bytes 589828
  3.5 1.0 %copy-start.2 = (bf16[144,256]{1,0:T(8,128)(2,1)S(1)}, bf16[144,256]{1,0:T(8,128)(2,1)}, u32[]{:S(2)}) copy-start(bf16[144,256]{1,0:T(8,128)(2,1)} %weight_ref.1) | copy-start | bytes 221188

commit v2 on v1

--- a/solution.py
+++ b/solution.py
@@ -3,7 +3,6 @@
 
 import jax
 import jax.numpy as jnp
-import numpy as np
 from jax import lax
 from jax.experimental import pallas as pl
 from jax.experimental.pallas import tpu as pltpu
@@ -166,14 +165,27 @@
 
 
 MESH = pl.DeviceIdType.MESH
-COPIES = 30
-WZ, WX, WS, WD, EX, GX, R1, X2, Z3 = 0, 3, 7, 11, 15, 18, 21, 23, 27
-
-
-def one_hot(index_column, width):
-    rows = index_column.shape[0]
-    lanes = lax.broadcasted_iota(jnp.int32, (rows, width), 1)
-    return jnp.where(index_column == lanes, 1.0, 0.0)
+COPIES = 45
+WZ, WX, WS, WD, EX, GX, R1, X2, Z3 = 0, 3, 7, 11, 15, 24, 33, 38, 42
+
+
+def lane_numbers(width):
+    return lax.broadcasted_iota(jnp.int32, (1, width), 1)
+
+
+def placing(row_of_lane, rows):
+    width = row_of_lane.shape[1]
+    numbers = lax.broadcasted_iota(jnp.int32, (rows, width), 0)
+    return jnp.where(numbers == row_of_lane, 1.0, 0.0).astype(jnp.bfloat16)
+
+
+def store_kernel(act_ref, in_grad_ref, w_grad_ref, act_out, in_grad_out, w_grad_out, sems):
+    pairs = ((act_ref, act_out), (in_grad_ref, in_grad_out), (w_grad_ref, w_grad_out))
+    copies = [pltpu.make_async_copy(a, b, sems.at[i]) for i, (a, b) in enumerate(pairs)]
+    for copy in copies:
+        copy.start()
+    for copy in copies:
+        copy.wait()
 
 
 def fused_kernel(
@@ -182,15 +194,14 @@
     fields_ref,
     weight_ref,
     cot_ref,
-    pad_index_ref,
-    cell_index_ref,
+    adjacency_ref,
     act_ref,
     in_grad_ref,
     w_grad_ref,
     full_w,
     edges,
     grad_edges,
-    pick,
+    cross,
     padded,
     shifted,
     total,
@@ -237,13 +248,46 @@
     def w_block(t, m):
         return full_w.at[pl.ds(pl.multiple_of((t * 4 + m) * block, 16), block)]
 
+    def edge_parts(buf, first, source, target):
+        top = (source == 0) | (target == source - 1)
+        bottom = (source == 3) | (target == source + 1)
+        spans = ((0, side, None), (side, line, top), (side + line, line, bottom))
+        for part, (start, count, needed) in enumerate(spans):
+            piece = buf.at[source, pl.ds(start, count)]
+            yield needed, piece, first + part
+
+    def when(needed, action):
+        if needed is None:
+            action()
+        else:
+            pl.when(needed)(action)
+
+    def each_edge(buf, first, incoming, action):
+        for k, t in enumerate(tile_peers):
+            source, target = (t, me) if incoming else (me, t)
+            for needed, piece, sem in edge_parts(buf, first + 3 * k, source, target):
+                when(needed, functools.partial(action, remote(piece, piece, sem, tile_id(t))))
+
+    def send_edges(buf, first):
+        each_edge(buf, first, False, lambda copy: copy.start())
+
+    def take_edges(buf, first):
+        each_edge(buf, first, True, lambda copy: copy.wait_recv())
+
+    def finish_edges(buf, first):
+        each_edge(buf, first, False, lambda copy: copy.wait_send())
+
     barrier = pltpu.get_barrier_semaphore()
     for t in tile_peers:
         pl.semaphore_signal(barrier, inc=1, device_id=tile_id(t), device_id_type=MESH)
     for k in range(1, 4):
         pl.semaphore_signal(barrier, inc=1, device_id=member_id(k), device_id_type=MESH)
 
-    side_pick = one_hot(cell_index_ref[0:side, 5:6], cells).astype(bf16)
+    row_start = me * band
+    q = lane_numbers(cells)
+    col, row, face = q % size, (q // size) % band, q // (size * band)
+    target = face * (2 * band) + row + jnp.where(col == 0, 0, band)
+    side_pick = placing(jnp.where((col == 0) | (col == size - 1), target, -1), side)
 
     def own_edges(values, out):
         cube = values.reshape(faces, band, size, channels)
@@ -263,8 +307,7 @@
 
     for k in (2, 1, 3):
         go(remote(w_block(me, z), w_block(me, z), WZ + k - 1, member_id(k)))
-    for k, t in enumerate(tile_peers):
-        go(remote(edges.at[me], edges.at[me], EX + k, tile_id(t)))
+    send_edges(edges, EX)
 
     def w_spread(k):
         part = w_block(me, (z + 4 - k) % 4)
@@ -274,8 +317,26 @@
         go(remote(part, part, WS + k, tile_id(sib)))
 
     w_spread(0)
-    for dx in range(3):
-        pick[dx] = one_hot(pad_index_ref[:, dx : dx + 1], 4 * side + 2 * line).astype(bf16)
+    q = lane_numbers(4 * line)
+    bank, along = q // size, q % size
+    base, turned = jnp.zeros_like(q), jnp.zeros_like(q)
+    for f in range(faces):
+        for e in range(4):
+            first = 3 * (4 * f + e)
+            here = bank == e * faces + f
+            start = adjacency_ref[first + 1] * line + adjacency_ref[first] * size
+            base = jnp.where(here, start, base)
+            turned = jnp.where(here, adjacency_ref[first + 2], turned)
+    cross[...] = placing(base + along + turned * (size - 1 - 2 * along), 4 * line)
+    q = lane_numbers(4 * side)
+    band_of, rest = q // side, q % side
+    order = placing(
+        ((rest // band) % 2) * line
+        + (rest // (2 * band)) * size
+        + band_of * band
+        + rest % band,
+        2 * line,
+    )
     for k in (1, 3, 2):
         w_spread(k)
 
@@ -290,27 +351,41 @@
             return jnp.where(columns(rows) == 0, 0.0, pltpu.roll(values, 1, 0))
         return jnp.where(columns(rows) == size - 1, 0.0, pltpu.roll(values, rows - 1, 0))
 
-    def with_halo(values, buf):
+    def with_halo(values, buf, north, south):
         above = buf[jnp.maximum(me - 1, 0), side + line : side + 2 * line].astype(f32)
         below = buf[jnp.minimum(me + 1, 3), side : side + line].astype(f32)
-        above = jnp.where(me > 0, above, 0.0).reshape(faces, 1, size, channels)
-        below = jnp.where(me < 3, below, 0.0).reshape(faces, 1, size, channels)
+        above = jnp.where(me > 0, above, north).reshape(faces, 1, size, channels)
+        below = jnp.where(me < 3, below, south).reshape(faces, 1, size, channels)
         own = values.astype(f32).reshape(faces, band, size, channels)
         return jnp.concatenate([above, own, below], axis=1).reshape(-1, channels)
 
     def lines_of(buf):
-        return jnp.concatenate(
-            [buf[t, 0:side] for t in range(4)]
-            + [buf[0, side : side + line], buf[3, side + line : side + 2 * line]],
-            axis=0,
-        )
-
-    for k, t in enumerate(tile_peers):
-        remote(edges.at[t], edges.at[t], EX + k, tile_id(t)).wait_recv()
-    lines = lines_of(edges)
-    center = with_halo(fields_ref[...], edges)
+        sides = jnp.concatenate([buf[t, 0:side] for t in range(4)], axis=0)
+        sides = jnp.dot(order, sides, preferred_element_type=f32).astype(bf16)
+        north = buf[0, side : side + line]
+        south = buf[3, side + line : side + 2 * line]
+        return jnp.concatenate([north, south, sides], axis=0)
+
+    take_edges(edges, EX)
+    cycle_cells = jnp.dot(cross[...], lines_of(edges), preferred_element_type=f32)
+    center = with_halo(
+        fields_ref[...], edges, cycle_cells[0:line], cycle_cells[line : 2 * line]
+    )
+    cycle_sides = cycle_cells[2 * line :].astype(bf16)
+    q = lane_numbers(line)
+    near = q % size - row_start + 1
+    spot = (q // size) * ((band + 2) * size) + near * size
+    inside = (near >= 0) & (near < band + 2)
     for dx in range(3):
-        values = moved(center, dx - 1) + jnp.dot(pick[dx], lines, preferred_element_type=f32)
+        values = moved(center, dx - 1)
+        if dx != 1:
+            first = line if dx else 0
+            put = placing(
+                jnp.where(inside, spot + (size - 1 if dx else 0), -1), faces * (band + 2) * size
+            )
+            values = values + jnp.dot(
+                put, cycle_sides[first : first + line], preferred_element_type=f32
+            )
         padded[dx] = values.astype(bf16).reshape(faces, band + 2, size, channels)
 
     for k in (0, 1, 3, 2):
@@ -342,8 +417,7 @@
     )
     act_grad = (cot_ref[...].astype(f32) * slope).astype(bf16)
     own_edges(act_grad, grad_edges)
-    for k, t in enumerate(tile_peers):
-        go(remote(grad_edges.at[me], grad_edges.at[me], GX + k, tile_id(t)))
+    send_edges(grad_edges, GX)
 
     for dy in range(3):
         for dx in range(3):
@@ -363,20 +437,23 @@
     def row_at(t, m):
         return pl.ds(pl.multiple_of((t * 4 + m) * block, 16), block)
 
-    go(remote(outgoing.at[quarter_at(diag)], from_core.at[0], R1, tile_id(sib)))
-    go(remote(outgoing.at[quarter_at(sib)], from_core.at[1], R1 + 1, tile_id(sib)))
-
-    remote(from_core.at[0], from_core.at[0], R1, tile_id(sib)).wait_recv()
     for k in (2, 1, 3, 0):
         m = (z + k) % 4
+        there = from_core.at[0, part_at(m)]
+        go(remote(outgoing.at[row_at(diag, m)], there, R1 + k, tile_id(sib)))
+    go(remote(outgoing.at[quarter_at(sib)], from_core.at[1], R1 + 4, tile_id(sib)))
+
+    for k in (2, 1, 3, 0):
+        m = (z + k) % 4
+        there = from_core.at[0, part_at(m)]
+        remote(there, there, R1 + k, tile_id(sib)).wait_recv()
         to_x[part_at(m)] = (
             total[row_at(across, m)] + from_core[0, part_at(m)].astype(f32)
         ).astype(bf16)
         go(remote(to_x.at[part_at(m)], from_x.at[part_at(m)], X2 + k, tile_id(across)))
 
-    for k, t in enumerate(tile_peers):
-        remote(grad_edges.at[t], grad_edges.at[t], GX + k, tile_id(t)).wait_recv()
-    center = with_halo(act_grad, grad_edges)
+    take_edges(grad_edges, GX)
+    center = with_halo(act_grad, grad_edges, 0.0, 0.0)
     for dx in range(3):
         shifted[dx] = (
             moved(center, 1 - dx).astype(bf16).reshape(faces, band + 2, size, channels)
@@ -392,7 +469,7 @@
                 preferred_element_type=f32,
             )
 
-    remote(from_core.at[1], from_core.at[1], R1 + 1, tile_id(sib)).wait_recv()
+    remote(from_core.at[1], from_core.at[1], R1 + 4, tile_id(sib)).wait_recv()
     for k in (2, 1, 3, 0):
         m = (z + k) % 4
         remote(to_x.at[part_at(m)], from_x.at[part_at(m)], X2 + k, tile_id(across)).wait_recv()
@@ -407,15 +484,8 @@
         else:
             w_grad_ref[...] = mine
 
-    lines = lines_of(grad_edges)
-    taps = [
-        jnp.dot(
-            one_hot(cell_index_ref[:, 2 + s : 3 + s], 4 * side + 2 * line).astype(bf16),
-            lines,
-            preferred_element_type=f32,
-        ).astype(bf16)
-        for s in range(3)
-    ]
+    lines = lines_of(grad_edges).astype(f32)
+    taps = [moved(lines, 1 - s).astype(bf16) for s in range(3)]
     pieces = []
     for edge in range(4):
         piece = jnp.zeros((line, channels), f32)
@@ -429,13 +499,26 @@
             )
         pieces.append(piece)
     cycle = jnp.concatenate(pieces, axis=0)
-    route = (
-        one_hot(cell_index_ref[:, 0:1], 4 * line) + one_hot(cell_index_ref[:, 1:2], 4 * line)
-    ).astype(bf16)
     high = cycle.astype(bf16)
     low = (cycle - high.astype(f32)).astype(bf16)
-    grad = grad + jnp.dot(route, high, preferred_element_type=f32)
-    grad = grad + jnp.dot(route, low, preferred_element_type=f32)
+    q = lane_numbers(2 * line)
+    lane_face, near = (q // size) % faces, q % size - row_start
+    spot = lane_face * (band * size) + near * size + jnp.where(q < line, 0, size - 1)
+    put = placing(jnp.where((near >= 0) & (near < band), spot, -1), cells)
+    grad = grad.reshape(faces, band, size, channels)
+    line_grad = jnp.zeros((4 * line, channels), f32)
+    side_grad = jnp.zeros((cells, channels), f32)
+    for level in (high, low):
+        routed = jnp.dot(cross[...], level, preferred_element_type=f32)
+        line_grad = line_grad + routed
+        side_grad = side_grad + jnp.dot(
+            put, routed[2 * line :].astype(bf16), preferred_element_type=f32
+        )
+    north = jnp.where(me == 0, line_grad[0:line], 0.0).reshape(faces, 1, size, channels)
+    south = jnp.where(me == 3, line_grad[line : 2 * line], 0.0).reshape(faces, 1, size, channels)
+    inner = jnp.zeros((faces, band - 2, size, channels), f32)
+    grad = grad + jnp.concatenate([north, inner, south], axis=1)
+    grad = grad.reshape(cells, channels) + side_grad
     in_grad_ref[...] = grad.astype(bf16)
 
     result = w_grad_ref[...]
@@ -443,57 +526,10 @@
         remote(from_z.at[k - 1], from_z.at[k - 1], Z3 + k - 1, member_id(k)).wait_recv()
         result = result + from_z[k - 1].astype(f32)
     w_grad_ref[...] = result * scale
+    finish_edges(edges, EX)
+    finish_edges(grad_edges, GX)
     for copy in started:
         copy.wait_send()
-
-
-def index_tables(adjacency, faces, band, size):
-    position = lax.axis_index("tile")
-    face, edge, flag = (adjacency[:, :, i][:, :, None] for i in range(3))
-    along = jnp.arange(size, dtype=jnp.int32)[None, None, :]
-    u = jnp.where(flag == 1, size - 1 - along, along)
-    side, line = faces * 2 * band, faces * size
-    on_rows = 4 * side + edge * line + face * size + u
-    on_sides = (u // band) * side + face * 2 * band + (edge - 2) * band + u % band
-    source = jnp.where(edge < 2, on_rows, on_sides)
-    cycle = edge * line + face * size + u
-
-    def framed(values, inner):
-        middle = jnp.full((faces, size, inner), -1, jnp.int32)
-        return jnp.concatenate([values[:, 2][:, :, None], middle, values[:, 3][:, :, None]], axis=2)
-
-    def ended(values):
-        return jnp.pad(values, ((0, 0), (1, 1)), constant_values=-1)[:, None]
-
-    whole = jnp.concatenate([ended(source[:, 0]), framed(source, size), ended(source[:, 1])], axis=1)
-    rows = lax.dynamic_slice_in_dim(whole, position * band, band + 2, 1)
-    pad_index = jnp.stack([rows[:, :, dx : dx + size] for dx in range(3)], axis=-1).reshape(-1, 3)
-    by_column = framed(cycle, size - 2)
-    by_row = jnp.concatenate(
-        [
-            cycle[:, 0][:, None],
-            jnp.full((faces, size - 2, size), -1, jnp.int32),
-            cycle[:, 1][:, None],
-        ],
-        axis=1,
-    )
-    both = jnp.stack([by_column, by_row], axis=-1)
-    both = lax.dynamic_slice_in_dim(both, position * band, band, 1).reshape(-1, 2)
-
-    e, f, t = np.meshgrid(np.arange(4), np.arange(faces), np.arange(size), indexing="ij")
-    fixed = np.full((faces * band * size, 4), -1, np.int32)
-    for s in range(3):
-        v = t + 1 - s
-        at = np.where(
-            e < 2,
-            4 * side + e * line + f * size + v,
-            (v // band) * side + f * 2 * band + (e - 2) * band + v % band,
-        )
-        fixed[:, s] = np.where((v < 0) | (v >= size), -1, at).reshape(-1)
-    f, k, r = np.meshgrid(np.arange(faces), np.arange(2), np.arange(band), indexing="ij")
-    fixed[:side, 3] = (f * band * size + r * size + k * (size - 1)).reshape(-1)
-    cell_index = jnp.concatenate([both, jnp.asarray(fixed)], axis=1)
-    return pad_index, cell_index
 
 
 def shards(fields, weight, cotangent, adjacency):
@@ -504,27 +540,25 @@
     if not (fits and size == 16 and block % 16 == 0 and (faces * 2 * band) % 16 == 0):
         return plain_shards(fields, weight, cotangent, adjacency)
     cells = faces * band * size
-    pad_index, cell_index = index_tables(adjacency, faces, band, size)
     side, line = faces * 2 * band, faces * size
     bf16, f32 = jnp.bfloat16, jnp.float32
     scale = 1.0 / math.sqrt(cells * tiles * across)
     rows = block * tiles * across
     whole = pl.BlockSpec(memory_space=pltpu.VMEM)
-    lines = 4 * side + 2 * line
-    act, in_grad, w_grad = pl.pallas_call(
+    results = pl.pallas_call(
         functools.partial(fused_kernel, (faces, band, size, channels), scale),
         out_shape=(
             jax.ShapeDtypeStruct((cells, channels), bf16),
             jax.ShapeDtypeStruct((cells, channels), bf16),
             jax.ShapeDtypeStruct((block, channels), f32),
         ),
-        in_specs=[whole] * 5,
+        in_specs=[whole] * 3 + [pl.BlockSpec(memory_space=pltpu.SMEM)],
         out_specs=(whole,) * 3,
         scratch_shapes=[
             pltpu.VMEM((rows, channels), bf16),
             pltpu.VMEM((4, side + 2 * line, channels), bf16),
             pltpu.VMEM((4, side + 2 * line, channels), bf16),
-            pltpu.VMEM((3, faces * (band + 2) * size, lines), bf16),
+            pltpu.VMEM((4 * line, 4 * line), bf16),
             pltpu.VMEM((3, faces, band + 2, size, channels), bf16),
             pltpu.VMEM((3, faces, band + 2, size, channels), bf16),
             pltpu.VMEM((rows, channels), f32),
@@ -544,9 +578,16 @@
         fields.reshape(cells, channels),
         weight,
         cotangent.reshape(cells, channels),
-        pad_index,
-        cell_index,
-    )
+        adjacency.reshape(-1),
+    )
+    anywhere = pl.BlockSpec(memory_space=pl.ANY)
+    act, in_grad, w_grad = pl.pallas_call(
+        store_kernel,
+        out_shape=tuple(jax.ShapeDtypeStruct(r.shape, r.dtype) for r in results),
+        in_specs=[whole] * 3,
+        out_specs=(anywhere,) * 3,
+        scratch_shapes=[pltpu.SemaphoreType.DMA((3,))],
+    )(*results)
     return act.reshape(fields.shape), in_grad.reshape(fields.shape), w_grad
 
 

time: 45 us -> 42.7 us (0.949)
  Pallas kernels: 38.3 us -> 36.1 us
    pallas_call x1, Pallas kernels: 38.3 us -> 34.2 us  [shards(): pl.pallas_call(functools.partial(fused_kernel, (faces, band, size, channe...]
    pallas_call x0 -> x1, Pallas kernels: none -> 1.91 us  [shards(): pl.pallas_call(store_kernel, out_shape=tuple((jax.ShapeDtypeStruct(r.shap...]
    unnamed x13, local copies, waits for them, and re-layouts: 4.04 us -> 5.53 us
    another operation x8 -> x0, local copies, waits for them, and re-layouts: 0.7 us -> none  [the longest x4 0.41 us: index_tables(): jnp.stack([rows[:, :, dx:dx + size] for dx in range(3)], axis=-1)]
where the time goes in v2:
time: 42.7 us; the launch traced here: 42.4 us
  Pallas kernels  36.1 us (85%)
  local copies, waits for them, and re-layouts  5.63 us (13%)
  between operations  0.66 us (2%)
    pallas_call x1, Pallas kernels, shards(): pl.pallas_call(functools.partial(fused_kernel, (faces, band, size, channe...  34.2 us
    unnamed x13, local copies, waits for them, and re-layouts  5.53 us
    pallas_call x1, Pallas kernels, shards(): pl.pallas_call(store_kernel, out_shape=tuple((jax.ShapeDtypeStruct(r.shap...  1.91 us

profile of v2, /device:TPU:0, one launch (start us, length us, event | category | flops | bytes accessed | tf_op | source)
XLA Modules:
  0.0 42.4 jit_solution(8092004037691908732)
XLA Ops:
  0.6 0.8 %copy.8 = s32[6,4,3]{2,1,0:T(4,128)S(1)} copy(s32[6,4,3]{0,1,2:T(4,128)} %param.7) | data formatting | bytes 576 | tf_op args[3]
  1.4 0.1 reshape.23.adjacency_ref
  1.5 0.0 copy-start
  1.5 0.9 %copy-done = bf16[1,6,4,16,256]{4,3,2,1,0:T(8,128)(2,1)S(1)} copy-done((bf16[1,6,4,16,256]{4,3,2,1,0:T(8,128)(2,1)S(1)}, bf16[1,6,4,16,256]{4,3,2,1,0:T(8,128)(2,1)}, u32[]{:S(2)}) %copy-start) | copy-done | bytes 196632
  2.5 0.0 copy-start.1
  2.5 0.9 %copy-done.1 = bf16[1,6,4,16,256]{4,3,2,1,0:T(8,128)(2,1)S(1)} copy-done((bf16[1,6,4,16,256]{4,3,2,1,0:T(8,128)(2,1)S(1)}, bf16[1,6,4,16,256]{4,3,2,1,0:T(8,128)(2,1)}, u32[]{:S(2)}) %copy-start.1) | copy-done | bytes 196632
  3.4 0.0 copy-start.5
  3.4 0.9 %copy-done.5 = bf16[144,256]{1,0:T(8,128)(2,1)S(1)} copy-done((bf16[144,256]{1,0:T(8,128)(2,1)S(1)}, bf16[144,256]{1,0:T(8,128)(2,1)}, u32[]{:S(2)}) %copy-start.5) | copy-done | bytes 73752
  4.3 34.2 %shard_map.67 = (bf16[384,256]{1,0:T(8,128)(2,1)S(1)}, bf16[384,256]{1,0:T(8,128)(2,1)S(1)}, f32[144,256]{1,0:T(8,128)S(1)}) custom-call(bf16[384,256]{1,0:T(8,128)(2,1)S(1)} %bitcast.4, bf16[144,256]{1,0:T(8,128)(2,1)S(1)} %copy-done.5, bf16[384,256]{1,0:T(8,128)(2,1)S(1)} %bitcast.5, s32[72]{0:T(128)S(1)} %reshape.23.adjacency_ref), custom_call_target="tpu_custom_call" | custom-call | tf_op jit(solution)/shard_map/pallas_call | solution.py:548
  38.5 0.0 copy-start.2
  38.5 0.7 %copy-done.2 = bf16[384,256]{1,0:T(8,128)(2,1)} copy-done((bf16[384,256]{1,0:T(8,128)(2,1)}, bf16[384,256]{1,0:T(8,128)(2,1)S(1)}, u32[]{:S(2)}) %copy-start.2) | copy-done | bytes 196632
  39.2 0.0 copy-start.3
  39.2 0.7 %copy-done.3 = bf16[384,256]{1,0:T(8,128)(2,1)} copy-done((bf16[384,256]{1,0:T(8,128)(2,1)}, bf16[384,256]{1,0:T(8,128)(2,1)S(1)}, u32[]{:S(2)}) %copy-start.3) | copy-done | bytes 196632
  39.8 0.0 copy-start.4
  39.9 0.7 %copy-done.4 = f32[144,256]{1,0:T(8,128)} copy-done((f32[144,256]{1,0:T(8,128)}, f32[144,256]{1,0:T(8,128)S(1)}, u32[]{:S(2)}) %copy-start.4) | copy-done | bytes 147480
  40.5 1.9 %shard_map.68 = (bf16[384,256]{1,0:T(8,128)(2,1)}, bf16[384,256]{1,0:T(8,128)(2,1)}, f32[144,256]{1,0:T(8,128)}) custom-call(bf16[384,256]{1,0:T(8,128)(2,1)} %copy-done.2, bf16[384,256]{1,0:T(8,128)(2,1)} %copy-done.3, f32[144,256]{1,0:T(8,128)} %copy-done.4), custom_call_target="tpu_custom_call" | custom-call | tf_op jit(solution)/shard_map/pallas_call | solution.py:584
Async XLA Ops:
  1.5 0.9 %copy-start = (bf16[1,6,4,16,256]{4,3,2,1,0:T(8,128)(2,1)S(1)}, bf16[1,6,4,16,256]{4,3,2,1,0:T(8,128)(2,1)}, u32[]{:S(2)}) copy-start(bf16[1,6,4,16,256]{4,3,2,1,0:T(8,128)(2,1)} %param.4) | copy-start | bytes 589828
  2.5 0.9 %copy-start.1 = (bf16[1,6,4,16,256]{4,3,2,1,0:T(8,128)(2,1)S(1)}, bf16[1,6,4,16,256]{4,3,2,1,0:T(8,128)(2,1)}, u32[]{:S(2)}) copy-start(bf16[1,6,4,16,256]{4,3,2,1,0:T(8,128)(2,1)} %param.6) | copy-start | bytes 589828
  3.4 0.9 %copy-start.5 = (bf16[144,256]{1,0:T(8,128)(2,1)S(1)}, bf16[144,256]{1,0:T(8,128)(2,1)}, u32[]{:S(2)}) copy-start(bf16[144,256]{1,0:T(8,128)(2,1)} %weight_ref.1) | copy-start | bytes 221188
  38.5 0.7 %copy-start.2 = (bf16[384,256]{1,0:T(8,128)(2,1)}, bf16[384,256]{1,0:T(8,128)(2,1)S(1)}, u32[]{:S(2)}) copy-start(bf16[384,256]{1,0:T(8,128)(2,1)S(1)} %get-tuple-element.9.act_ref) | copy-start | bytes 589828
  39.2 0.7 %copy-start.3 = (bf16[384,256]{1,0:T(8,128)(2,1)}, bf16[384,256]{1,0:T(8,128)(2,1)S(1)}, u32[]{:S(2)}) copy-start(bf16[384,256]{1,0:T(8,128)(2,1)S(1)} %get-tuple-element.10.in_grad_ref) | copy-start | bytes 589828
  39.8 0.7 %copy-start.4 = (f32[144,256]{1,0:T(8,128)}, f32[144,256]{1,0:T(8,128)S(1)}, u32[]{:S(2)}) copy-start(f32[144,256]{1,0:T(8,128)S(1)} %get-tuple-element.11.w_grad_ref) | copy-start | bytes 442372

commit v3 on v2

--- a/solution.py
+++ b/solution.py
@@ -191,13 +191,18 @@
 def fused_kernel(
     dims,
     scale,
-    fields_ref,
-    weight_ref,
-    cot_ref,
+    fields_hbm,
+    weight_hbm,
+    cot_hbm,
     adjacency_ref,
+    act_hbm,
+    in_grad_hbm,
+    w_grad_hbm,
     act_ref,
     in_grad_ref,
     w_grad_ref,
+    fields_ref,
+    cot_ref,
     full_w,
     edges,
     grad_edges,
@@ -213,12 +218,13 @@
     from_z,
     send_sem,
     recv_sem,
+    load_sem,
 ):
     faces, band, size, channels = dims
     cells = faces * band * size
     line = faces * size
     side = faces * 2 * band
-    block = weight_ref.shape[0]
+    block = weight_hbm.shape[0]
     quarter = 4 * block
     f32, bf16 = jnp.float32, jnp.bfloat16
     me = lax.axis_index("tile")
@@ -277,6 +283,12 @@
     def finish_edges(buf, first):
         each_edge(buf, first, False, lambda copy: copy.wait_send())
 
+    load_w = pltpu.make_async_copy(weight_hbm, w_block(me, z), load_sem.at[0])
+    load_fields = pltpu.make_async_copy(fields_hbm, fields_ref, load_sem.at[1])
+    load_cot = pltpu.make_async_copy(cot_hbm, cot_ref, load_sem.at[2])
+    for load in (load_w, load_fields, load_cot):
+        load.start()
+
     barrier = pltpu.get_barrier_semaphore()
     for t in tile_peers:
         pl.semaphore_signal(barrier, inc=1, device_id=tile_id(t), device_id_type=MESH)
@@ -295,8 +307,7 @@
         out[me, side : side + line] = cube[:, 0].reshape(line, channels)
         out[me, side + line : side + 2 * line] = cube[:, band - 1].reshape(line, channels)
 
-    w_block(me, z)[...] = weight_ref[...]
-    own_edges(fields_ref[...], edges)
+    load_w.wait()
     pl.semaphore_wait(barrier, 6)
 
     started = []
@@ -307,6 +318,8 @@
 
     for k in (2, 1, 3):
         go(remote(w_block(me, z), w_block(me, z), WZ + k - 1, member_id(k)))
+    load_fields.wait()
+    own_edges(fields_ref[...], edges)
     send_edges(edges, EX)
 
     def w_spread(k):
@@ -322,11 +335,10 @@
     base, turned = jnp.zeros_like(q), jnp.zeros_like(q)
     for f in range(faces):
         for e in range(4):
-            first = 3 * (4 * f + e)
             here = bank == e * faces + f
-            start = adjacency_ref[first + 1] * line + adjacency_ref[first] * size
+            start = adjacency_ref[1, e, f] * line + adjacency_ref[0, e, f] * size
             base = jnp.where(here, start, base)
-            turned = jnp.where(here, adjacency_ref[first + 2], turned)
+            turned = jnp.where(here, adjacency_ref[2, e, f], turned)
     cross[...] = placing(base + along + turned * (size - 1 - 2 * along), 4 * line)
     q = lane_numbers(4 * side)
     band_of, rest = q // side, q % side
@@ -409,9 +421,12 @@
     for dy in range(3):
         for dx in range(3):
             pre = pre + jnp.dot(window(dy, dx), w_of(dy, dx), preferred_element_type=f32)
+    load_cot.wait()
     square = pre * pre
     bend = jnp.tanh(gelu_scale * (pre + 0.044715 * pre * square))
     act_ref[...] = (0.5 * pre * (1.0 + bend)).astype(bf16)
+    keep_act = pltpu.make_async_copy(act_ref, act_hbm, load_sem.at[3])
+    keep_act.start()
     slope = 0.5 * (1.0 + bend) + 0.5 * pre * (1.0 - bend * bend) * (
         gelu_scale * (1.0 + 3 * 0.044715 * square)
     )
@@ -520,16 +535,23 @@
     grad = grad + jnp.concatenate([north, inner, south], axis=1)
     grad = grad.reshape(cells, channels) + side_grad
     in_grad_ref[...] = grad.astype(bf16)
+    keep_grad = pltpu.make_async_copy(in_grad_ref, in_grad_hbm, load_sem.at[4])
+    keep_grad.start()
 
     result = w_grad_ref[...]
     for k in range(1, 4):
         remote(from_z.at[k - 1], from_z.at[k - 1], Z3 + k - 1, member_id(k)).wait_recv()
         result = result + from_z[k - 1].astype(f32)
     w_grad_ref[...] = result * scale
+    keep_w = pltpu.make_async_copy(w_grad_ref, w_grad_hbm, load_sem.at[5])
+    keep_w.start()
     finish_edges(edges, EX)
     finish_edges(grad_edges, GX)
     for copy in started:
         copy.wait_send()
+    keep_act.wait()
+    keep_grad.wait()
+    keep_w.wait()
 
 
 def shards(fields, weight, cotangent, adjacency):
@@ -544,7 +566,7 @@
     bf16, f32 = jnp.bfloat16, jnp.float32
     scale = 1.0 / math.sqrt(cells * tiles * across)
     rows = block * tiles * across
-    whole = pl.BlockSpec(memory_space=pltpu.VMEM)
+    anywhere = pl.BlockSpec(memory_space=pl.ANY)
     results = pl.pallas_call(
         functools.partial(fused_kernel, (faces, band, size, channels), scale),
         out_shape=(
@@ -552,9 +574,14 @@
             jax.ShapeDtypeStruct((cells, channels), bf16),
             jax.ShapeDtypeStruct((block, channels), f32),
         ),
-        in_specs=[whole] * 3 + [pl.BlockSpec(memory_space=pltpu.SMEM)],
-        out_specs=(whole,) * 3,
+        in_specs=[anywhere] * 3 + [pl.BlockSpec(memory_space=pltpu.SMEM)],
+        out_specs=(anywhere,) * 3,
         scratch_shapes=[
+            pltpu.VMEM((cells, channels), bf16),
+            pltpu.VMEM((cells, channels), bf16),
+            pltpu.VMEM((block, channels), f32),
+            pltpu.VMEM((cells, channels), bf16),
+            pltpu.VMEM((cells, channels), bf16),
             pltpu.VMEM((rows, channels), bf16),
             pltpu.VMEM((4, side + 2 * line, channels), bf16),
             pltpu.VMEM((4, side + 2 * line, channels), bf16),
@@ -570,23 +597,24 @@
             pltpu.VMEM((3, block, channels), bf16),
             pltpu.SemaphoreType.DMA((COPIES,)),
             pltpu.SemaphoreType.DMA((COPIES,)),
+            pltpu.SemaphoreType.DMA((6,)),
         ],
         compiler_params=pltpu.CompilerParams(
-            collective_id=0, has_side_effects=True, vmem_limit_bytes=40 * 1024 * 1024
+            collective_id=0, has_side_effects=True, vmem_limit_bytes=60 * 1024 * 1024
         ),
     )(
         fields.reshape(cells, channels),
         weight,
         cotangent.reshape(cells, channels),
-        adjacency.reshape(-1),
-    )
-    anywhere = pl.BlockSpec(memory_space=pl.ANY)
+        adjacency.transpose(2, 1, 0),
+    )
     act, in_grad, w_grad = pl.pallas_call(
         store_kernel,
         out_shape=tuple(jax.ShapeDtypeStruct(r.shape, r.dtype) for r in results),
-        in_specs=[whole] * 3,
+        in_specs=[anywhere] * 3,
         out_specs=(anywhere,) * 3,
         scratch_shapes=[pltpu.SemaphoreType.DMA((3,))],
+        compiler_params=pltpu.CompilerParams(vmem_limit_bytes=60 * 1024 * 1024),
     )(*results)
     return act.reshape(fields.shape), in_grad.reshape(fields.shape), w_grad
 

time: 42.7 us -> 53.6 us (1.26)
  Pallas kernels: 36.1 us -> 52.7 us
  local copies, waits for them, and re-layouts: 5.63 us -> 0 us
    pallas_call x1, Pallas kernels: 1.91 us -> 17.5 us  [shards(): pl.pallas_call(store_kernel, out_shape=tuple((jax.ShapeDtypeStruct(r.shap...]
    unnamed x13 -> x0, local copies, waits for them, and re-layouts: 5.53 us -> none
    pallas_call x1, Pallas kernels: 34.2 us -> 35.2 us  [shards(): pl.pallas_call(functools.partial(fused_kernel, (faces, band, size, channe...]
where the time goes in v3:
time: 53.6 us; the launch traced here: 53.4 us
  Pallas kernels  52.7 us (98%)
  between operations  0.64 us (1%)
    pallas_call x1, Pallas kernels, shards(): pl.pallas_call(functools.partial(fused_kernel, (faces, band, size, channe...  35.2 us
    pallas_call x1, Pallas kernels, shards(): pl.pallas_call(store_kernel, out_shape=tuple((jax.ShapeDtypeStruct(r.shap...  17.5 us

profile of v3, /device:TPU:0, one launch (start us, length us, event | category | flops | bytes accessed | tf_op | source)
XLA Modules:
  0.0 53.4 jit_solution(17094890444159647285)
XLA Ops:
  0.6 35.2 %shard_map.67 = (bf16[384,256]{1,0:T(8,128)(2,1)}, bf16[384,256]{1,0:T(8,128)(2,1)}, f32[144,256]{1,0:T(8,128)}) custom-call(bf16[384,256]{1,0:T(8,128)(2,1)} %bitcast.5, bf16[144,256]{1,0:T(8,128)(2,1)} %weight_hbm.1, bf16[384,256]{1,0:T(8,128)(2,1)} %bitcast.6, s32[3,4,6]{2,1,0:T(4,128)} %bitcast.7), custom_call_target="tpu_custom_call" | custom-call | tf_op jit(solution)/shard_map/pallas_call | solution.py:570
  35.8 17.5 %shard_map.68 = (bf16[384,256]{1,0:T(8,128)(2,1)}, bf16[384,256]{1,0:T(8,128)(2,1)}, f32[144,256]{1,0:T(8,128)}) custom-call(bf16[384,256]{1,0:T(8,128)(2,1)} %get-tuple-element.9.act_ref, bf16[384,256]{1,0:T(8,128)(2,1)} %get-tuple-element.10.in_grad_ref, f32[144,256]{1,0:T(8,128)} %get-tuple-element.11.w_grad_ref), custom_call_target="tpu_custom_call" | custom-call | tf_op jit(solution)/shard_map/pallas_call | solution.py:611

commit v4 on v3

--- a/solution.py
+++ b/solution.py
@@ -179,13 +179,17 @@
     return jnp.where(numbers == row_of_lane, 1.0, 0.0).astype(jnp.bfloat16)
 
 
-def store_kernel(act_ref, in_grad_ref, w_grad_ref, act_out, in_grad_out, w_grad_out, sems):
-    pairs = ((act_ref, act_out), (in_grad_ref, in_grad_out), (w_grad_ref, w_grad_out))
-    copies = [pltpu.make_async_copy(a, b, sems.at[i]) for i, (a, b) in enumerate(pairs)]
-    for copy in copies:
-        copy.start()
-    for copy in copies:
-        copy.wait()
+def store_kernel(*refs):
+    sources, targets, staged, sems = refs[0:3], refs[3:6], refs[6:9], refs[9]
+    loads = [pltpu.make_async_copy(sources[i], staged[i], sems.at[i]) for i in range(3)]
+    stores = [pltpu.make_async_copy(staged[i], targets[i], sems.at[3 + i]) for i in range(3)]
+    for load in loads:
+        load.start()
+    for load, store in zip(loads, stores):
+        load.wait()
+        store.start()
+    for store in stores:
+        store.wait()
 
 
 def fused_kernel(
@@ -613,7 +617,8 @@
         out_shape=tuple(jax.ShapeDtypeStruct(r.shape, r.dtype) for r in results),
         in_specs=[anywhere] * 3,
         out_specs=(anywhere,) * 3,
-        scratch_shapes=[pltpu.SemaphoreType.DMA((3,))],
+        scratch_shapes=[pltpu.VMEM(r.shape, r.dtype) for r in results]
+        + [pltpu.SemaphoreType.DMA((6,))],
         compiler_params=pltpu.CompilerParams(vmem_limit_bytes=60 * 1024 * 1024),
     )(*results)
     return act.reshape(fields.shape), in_grad.reshape(fields.shape), w_grad

time: 53.6 us -> 37.9 us (0.71)
  Pallas kernels: 52.7 us -> 37 us
    pallas_call x1, Pallas kernels: 17.5 us -> 1.81 us  [shards(): pl.pallas_call(store_kernel, out_shape=tuple((jax.ShapeDtypeStruct(r.shap...]
where the time goes in v4:
time: 37.9 us; the launch traced here: 37.7 us
  Pallas kernels  37 us (98%)
  between operations  0.64 us (2%)
    pallas_call x1, Pallas kernels, shards(): pl.pallas_call(functools.partial(fused_kernel, (faces, band, size, channe...  35.2 us
    pallas_call x1, Pallas kernels, shards(): pl.pallas_call(store_kernel, out_shape=tuple((jax.ShapeDtypeStruct(r.shap...  1.81 us

profile of v4, /device:TPU:0, one launch (start us, length us, event | category | flops | bytes accessed | tf_op | source)
XLA Modules:
  0.0 37.7 jit_solution(17356542555565537116)
XLA Ops:
  0.6 35.2 %shard_map.67 = (bf16[384,256]{1,0:T(8,128)(2,1)}, bf16[384,256]{1,0:T(8,128)(2,1)}, f32[144,256]{1,0:T(8,128)}) custom-call(bf16[384,256]{1,0:T(8,128)(2,1)} %bitcast.5, bf16[144,256]{1,0:T(8,128)(2,1)} %weight_hbm.1, bf16[384,256]{1,0:T(8,128)(2,1)} %bitcast.6, s32[3,4,6]{2,1,0:T(4,128)} %bitcast.7), custom_call_target="tpu_custom_call" | custom-call | tf_op jit(solution)/shard_map/pallas_call | solution.py:574
  35.8 1.8 %shard_map.68 = (bf16[384,256]{1,0:T(8,128)(2,1)}, bf16[384,256]{1,0:T(8,128)(2,1)}, f32[144,256]{1,0:T(8,128)}) custom-call(bf16[384,256]{1,0:T(8,128)(2,1)} %get-tuple-element.9.refs_0_, bf16[384,256]{1,0:T(8,128)(2,1)} %get-tuple-element.10.refs_1_, f32[144,256]{1,0:T(8,128)} %get-tuple-element.11.refs_2_), custom_call_target="tpu_custom_call" | custom-call | tf_op jit(solution)/shard_map/pallas_call | solution.py:615

commit v5 on v4

--- a/solution.py
+++ b/solution.py
@@ -322,10 +322,6 @@
 
     for k in (2, 1, 3):
         go(remote(w_block(me, z), w_block(me, z), WZ + k - 1, member_id(k)))
-    load_fields.wait()
-    own_edges(fields_ref[...], edges)
-    send_edges(edges, EX)
-
     def w_spread(k):
         part = w_block(me, (z + 4 - k) % 4)
         if k:
@@ -334,6 +330,10 @@
         go(remote(part, part, WS + k, tile_id(sib)))
 
     w_spread(0)
+    load_fields.wait()
+    own_edges(fields_ref[...], edges)
+    send_edges(edges, EX)
+
     q = lane_numbers(4 * line)
     bank, along = q // size, q % size
     base, turned = jnp.zeros_like(q), jnp.zeros_like(q)
@@ -436,7 +436,6 @@
     )
     act_grad = (cot_ref[...].astype(f32) * slope).astype(bf16)
     own_edges(act_grad, grad_edges)
-    send_edges(grad_edges, GX)
 
     for dy in range(3):
         for dx in range(3):
@@ -470,6 +469,23 @@
             total[row_at(across, m)] + from_core[0, part_at(m)].astype(f32)
         ).astype(bf16)
         go(remote(to_x.at[part_at(m)], from_x.at[part_at(m)], X2 + k, tile_id(across)))
+
+    send_edges(grad_edges, GX)
+
+    remote(from_core.at[1], from_core.at[1], R1 + 4, tile_id(sib)).wait_recv()
+    for k in (2, 1, 3, 0):
+        m = (z + k) % 4
+        remote(to_x.at[part_at(m)], from_x.at[part_at(m)], X2 + k, tile_id(across)).wait_recv()
+        mine = (
+            total[row_at(me, m)]
+            + from_core[1, part_at(m)].astype(f32)
+            + from_x[part_at(m)].astype(f32)
+        )
+        if k:
+            to_z[k - 1] = mine.astype(bf16)
+            go(remote(to_z.at[k - 1], from_z.at[k - 1], Z3 + k - 1, member_id(k)))
+        else:
+            w_grad_ref[...] = mine
 
     take_edges(grad_edges, GX)
     center = with_halo(act_grad, grad_edges, 0.0, 0.0)
@@ -487,21 +503,6 @@
                 over_outputs,
                 preferred_element_type=f32,
             )
-
-    remote(from_core.at[1], from_core.at[1], R1 + 4, tile_id(sib)).wait_recv()
-    for k in (2, 1, 3, 0):
-        m = (z + k) % 4
-        remote(to_x.at[part_at(m)], from_x.at[part_at(m)], X2 + k, tile_id(across)).wait_recv()
-        mine = (
-            total[row_at(me, m)]
-            + from_core[1, part_at(m)].astype(f32)
-            + from_x[part_at(m)].astype(f32)
-        )
-        if k:
-            to_z[k - 1] = mine.astype(bf16)
-            go(remote(to_z.at[k - 1], from_z.at[k - 1], Z3 + k - 1, member_id(k)))
-        else:
-            w_grad_ref[...] = mine
 
     lines = lines_of(grad_edges).astype(f32)
     taps = [moved(lines, 1 - s).astype(bf16) for s in range(3)]

time: 37.9 us -> 38.2 us (level); the launches traced: 37.7 us -> 37.5 us
  no operation moved by 1% of the time
where the time goes in v5:
time: 38.2 us; the launch traced here: 37.5 us
  Pallas kernels  36.9 us (97%)
  between operations  0.64 us (2%)
    pallas_call x1, Pallas kernels, shards(): pl.pallas_call(functools.partial(fused_kernel, (faces, band, size, channe...  35.1 us
    pallas_call x1, Pallas kernels, shards(): pl.pallas_call(store_kernel, out_shape=tuple((jax.ShapeDtypeStruct(r.shap...  1.81 us

profile of v5, /device:TPU:0, one launch (start us, length us, event | category | flops | bytes accessed | tf_op | source)
XLA Modules:
  0.0 37.5 jit_solution(17271528672876208299)
XLA Ops:
  0.6 35.1 %shard_map.67 = (bf16[384,256]{1,0:T(8,128)(2,1)}, bf16[384,256]{1,0:T(8,128)(2,1)}, f32[144,256]{1,0:T(8,128)}) custom-call(bf16[384,256]{1,0:T(8,128)(2,1)} %bitcast.5, bf16[144,256]{1,0:T(8,128)(2,1)} %weight_hbm.1, bf16[384,256]{1,0:T(8,128)(2,1)} %bitcast.6, s32[3,4,6]{2,1,0:T(4,128)} %bitcast.7), custom_call_target="tpu_custom_call" | custom-call | tf_op jit(solution)/shard_map/pallas_call | solution.py:575
  35.7 1.8 %shard_map.68 = (bf16[384,256]{1,0:T(8,128)(2,1)}, bf16[384,256]{1,0:T(8,128)(2,1)}, f32[144,256]{1,0:T(8,128)}) custom-call(bf16[384,256]{1,0:T(8,128)(2,1)} %get-tuple-element.9.refs_0_, bf16[384,256]{1,0:T(8,128)(2,1)} %get-tuple-element.10.refs_1_, f32[144,256]{1,0:T(8,128)} %get-tuple-element.11.refs_2_), custom_call_target="tpu_custom_call" | custom-call | tf_op jit(solution)/shard_map/pallas_call | solution.py:616
